TPU v7x, 256 devices: a whole 4x4x8 slice. The times are simulated.
256 devices in a mesh: seq: 64 (over x_lo, z, y), tensor: 4 (over x_hi, core).
Axes of the slice: x: 4 (x_hi: 2, x_lo: 2; x = x_hi * 2 + x_lo), y: 4, z: 8, core: 2. Of those that a mesh axis runs over, the one named last changes fastest.
Arguments:
- queries: bfloat16 [16384, 2048], P('seq', 'tensor'), may hold values from -120 to 120
- key_heads: bfloat16 [16384, 2, 128], P('seq'), may hold values from -6 to 6
- value_heads: bfloat16 [16384, 2, 128], P('seq'), may hold values from -6 to 6
- doc_lengths: int32 [8], replicated, may hold values from 1 to 8448, 16384 in all
- out_weight: bfloat16 [2048, 8192], P('tensor'), may hold values from -0.75 to 0.75
Outputs:
- projected: bfloat16 [16384, 8192], P('seq', 'tensor')
Inputs may be any that keep to these rules, and one draw needn't show every extreme that they name: `doc_lengths`: they sum to 16384; the longest document has exactly 8448 tokens.
All inputs are finite; a program needn't handle non-finite values.
Results may differ from a plain program's by a relative error of at most 0.015.
Values may be sent and summed in bfloat16 or wider, within the bound.
No kernel may reach another device: no remote copies, remote signals or barrier semaphores. Data moves between devices by JAX's collectives and lax.ppermute only.
A program may use at most 192 MiB of HBM per device.

v0:
```python
import functools
import math

import jax
import jax.numpy as jnp
from jax import lax
from jax.experimental import pallas as pl
from jax.experimental.pallas import tpu as pltpu
from jax.sharding import PartitionSpec as P

HQ = 16
KVH = 2
HD = 128
SEQ = 64
TENSOR = 4
ROW = 4
THETA = 500000.0
EMPTY = -1e30
MASKED = -1e32
LOG2E = math.log2(math.e)
BLOCK = 256
ROW_TOKENS = ROW * BLOCK
HEADS = 8
LANES = HEADS * BLOCK
STATE = HD + 8
TILE = 512
NOWHERE = -(1 << 24)
OUT_COLUMNS = 2048
MIB = 1024 * 1024


def device_perm(move):
    pairs = []
    for s in range(SEQ):
        for hi in range(2):
            for core in range(2):
                to = move(s, hi, core)
                if to is not None:
                    pairs.append((s * TENSOR + hi * 2 + core, to[0] * TENSOR + to[1] * 2 + to[2]))
    return pairs


def permute(x, move):
    return lax.ppermute(x, ("seq", "tensor"), device_perm(move))


def in_row(shift):
    return lambda s, hi, core: (s - s % ROW + (s + shift) % ROW, hi, core)


def other_core(s, hi, core):
    return s, hi, 1 - core


def other_hi(s, hi, core):
    return s, 1 - hi, core


def far_block(s, hi, core):
    if core == 0 and s % ROW == ROW - 1 and s + 33 < SEQ:
        return s + 33, hi, core
    return None


def along_rows(step):
    def move(s, hi, core):
        if core == 0:
            return (s + step * ROW, hi, core) if s + step * ROW < SEQ else None
        return (s + (9 - step) * ROW) % SEQ, hi, core

    return move


def two_rows_on(s, hi, core):
    if core == 0:
        return (s + 2 * ROW, hi, core) if s + 2 * ROW < SEQ else None
    return (s - 2 * ROW) % SEQ, hi, core


def rope_tables(positions):
    half = HD // 2
    exponents = jnp.arange(half, dtype=jnp.float32) * (2.0 / HD)
    inverse = jnp.power(jnp.float32(THETA), -exponents)
    angles = positions.astype(jnp.float32)[:, None] * inverse[None, :]
    return jnp.cos(angles), jnp.sin(angles)


def rope(values, cosine, sine):
    half = HD // 2
    first, second = values[..., :half], values[..., half:]
    return jnp.concatenate(
        [first * cosine - second * sine, second * cosine + first * sine], axis=-1
    )


def place():
    s, t = lax.axis_index("seq"), lax.axis_index("tensor")
    return s, t >> 1, t & 1, s >> 2, s & 3


def part_at(kind, shift):
    s, _, core, row, col = place()
    at = (col + ROW - shift) & 3
    if kind == "far":
        there = (core == 0) & (col == 0) & (s >= 33)
        return jnp.where(there, (s - 33) * BLOCK, NOWHERE), BLOCK
    if kind == "half":
        base = (row * ROW + at) * BLOCK + core * (BLOCK // 2)
        return jnp.where(at > col, NOWHERE, base), BLOCK // 2
    return (jnp.where(core == 0, row - kind, row - 9 + kind) * ROW + at) * BLOCK, BLOCK


def attend_kernel(kinds, fresh, q_ref, low_ref, *rest):
    state = rest[-1]
    kept, refs = (None, rest[:-1]) if fresh else (rest[-2], rest[:-2])
    scale = HD**-0.5 * LOG2E
    first_query = place()[0] * BLOCK
    low_first = jnp.min(low_ref[0:1, 0:HD])
    parts, bases, none = [], [], True
    at, i = 0, 0
    for kind, shift in kinds:
        base, size = part_at(kind, shift)
        parts.append(refs[i].at[at : at + size])
        at += size
        if at == refs[i].shape[0]:
            at, i = 0, i + 1
        bases.append(base)
        none = (low_first >= base + size) & none

    def step():
        q = q_ref[...]
        low = low_ref[0:1, :]
        scores = []
        for part, base, kind in zip(parts, bases, kinds):
            s = jnp.dot(part[:, :HD], q, preferred_element_type=jnp.float32)
            at = lax.broadcasted_iota(jnp.int32, s.shape, 0)
            live = at >= low - base
            if kind == ("half", 0):
                query = lax.broadcasted_iota(jnp.int32, (1, LANES), 1) % BLOCK + first_query
                live = live & (at <= query - base)
            scores.append(jnp.where(live, s, MASKED))
        s = jnp.concatenate(scores, axis=0) if len(scores) > 1 else scores[0]
        values = [part[:, HD:].T for part in parts]
        values = jnp.concatenate(values, axis=1) if len(values) > 1 else values[0]
        values = jnp.concatenate([values, jnp.ones((16, values.shape[1]), jnp.bfloat16)], axis=0)
        peak = jnp.max(s, axis=0, keepdims=True) * scale
        old = jnp.full_like(peak, EMPTY) if fresh else kept[HD : HD + 1, :]
        new = jnp.maximum(old, peak)
        weights = jnp.exp2(s * scale - new).astype(jnp.bfloat16)
        summed = jnp.dot(values, weights, preferred_element_type=jnp.float32)
        denom = summed[HD : HD + 1]
        summed = summed[:HD]
        if not fresh:
            alpha = jnp.exp2(old - new)
            summed = summed + kept[:HD, :] * alpha
            denom = denom + kept[HD + 1 : HD + 2, :] * alpha
        state[:HD, :] = summed
        state[HD:, :] = jnp.concatenate([new, denom, jnp.zeros((6, LANES), jnp.float32)], axis=0)

    if fresh:
        step()
    else:

        @pl.when(none)
        def _():
            state[...] = kept[...]

        @pl.when(jnp.logical_not(none))
        def _():
            step()


def attend(q_all, low, refs, kinds, state=None):
    operands = list(refs) + ([] if state is None else [state])
    return pl.pallas_call(
        functools.partial(attend_kernel, kinds, state is None),
        out_shape=jax.ShapeDtypeStruct((STATE, LANES), jnp.float32),
        in_specs=[pl.BlockSpec(memory_space=pltpu.VMEM)] * (2 + len(operands)),
        out_specs=pl.BlockSpec(memory_space=pltpu.VMEM),
        input_output_aliases={} if state is None else {1 + len(operands): 0},
        compiler_params=pltpu.CompilerParams(vmem_limit_bytes=32 * MIB),
        cost_estimate=pl.CostEstimate(flops=1, bytes_accessed=1, transcendentals=0),
        name="attend",
    )(q_all, low, *operands)


def turn_kernel(queries, cosine, sine, out):
    half = HD // 2
    for h in range(queries.shape[1] // HD):
        x = queries[:, h * HD : (h + 1) * HD].astype(jnp.float32)
        turned = rope(x, cosine[...], sine[...]).astype(jnp.bfloat16)
        out[:, h * BLOCK : (h + 1) * BLOCK] = turned.T


def turn(queries, cosine, sine):
    return pl.pallas_call(
        turn_kernel,
        out_shape=jax.ShapeDtypeStruct((HD, queries.shape[1] // HD * BLOCK), jnp.bfloat16),
        in_specs=[pl.BlockSpec(memory_space=pltpu.VMEM)] * 3,
        out_specs=pl.BlockSpec(memory_space=pltpu.VMEM),
        compiler_params=pltpu.CompilerParams(vmem_limit_bytes=16 * MIB),
        cost_estimate=pl.CostEstimate(flops=1, bytes_accessed=1, transcendentals=0),
        name="turn",
    )(queries, cosine, sine)


def merged(mine, theirs, out):
    for h in range(HEADS):
        a = slice(h * BLOCK, (h + 1) * BLOCK)
        g = (h + HEADS // 2) % HEADS
        b = slice(g * BLOCK, (g + 1) * BLOCK)
        peak_a, peak_b = mine[HD : HD + 1, a], theirs[HD : HD + 1, b]
        peak = jnp.maximum(peak_a, peak_b)
        scale_a, scale_b = jnp.exp2(peak_a - peak), jnp.exp2(peak_b - peak)
        denom = mine[HD + 1 : HD + 2, a] * scale_a + theirs[HD + 1 : HD + 2, b] * scale_b
        summed = mine[:HD, a] * scale_a + theirs[:HD, b] * scale_b
        out[:, h * HD : (h + 1) * HD] = (summed / denom).T.astype(jnp.bfloat16)


def project_kernel(other_side, first, merging, *rest):
    half = HEADS * HD // 2
    _, hi, core, _, _ = place()
    weights, sems = rest[-2:]
    if merging:
        mine, theirs, own_weight, other_weight, attended = rest[:5]
        outs = rest[5:-2]
    else:
        attended, own_weight, other_weight = rest[:3]
        outs = rest[3:-2]
    at = (2 * (1 - hi if other_side else hi) + core) * OUT_COLUMNS + first
    pieces = weights.shape[0]
    for i in range(pieces):
        columns = pl.ds(pl.multiple_of(at + i * TILE, TILE), TILE)
        for j, weight in enumerate((own_weight, other_weight)):
            pltpu.make_async_copy(weight.at[:, columns], weights.at[i, j], sems.at[i, j]).start()
    if merging:
        merged(mine, theirs, attended)
    out, filled = 0, 0
    for i in range(pieces):
        columns = pl.ds(pl.multiple_of(at + i * TILE, TILE), TILE)
        for j, weight in enumerate((own_weight, other_weight)):
            pltpu.make_async_copy(weight.at[:, columns], weights.at[i, j], sems.at[i, j]).wait()
        total = jnp.dot(attended[:, :half], weights[i, 0], preferred_element_type=jnp.float32)
        total += jnp.dot(attended[:, half:], weights[i, 1], preferred_element_type=jnp.float32)
        outs[out][:, filled : filled + TILE] = total.astype(outs[out].dtype)
        filled += TILE
        if filled == outs[out].shape[1]:
            out, filled = out + 1, 0


def project(operands, weights, other_side, first, widths, dtype, merging=False):
    half = HEADS * HD // 2
    shapes = [jax.ShapeDtypeStruct((BLOCK, width), dtype) for width in widths]
    if merging:
        shapes = [jax.ShapeDtypeStruct((BLOCK, 2 * half), jnp.bfloat16)] + shapes
    pieces = sum(widths) // TILE
    vmem = pl.BlockSpec(memory_space=pltpu.VMEM)
    return pl.pallas_call(
        functools.partial(project_kernel, other_side, first, merging),
        out_shape=shapes,
        in_specs=[vmem] * len(operands)
        + [pl.BlockSpec(memory_space=pltpu.HBM)] * 2,
        out_specs=[vmem] * len(shapes),
        scratch_shapes=[
            pltpu.VMEM((pieces, 2, half, TILE), jnp.bfloat16),
            pltpu.SemaphoreType.DMA((pieces, 2)),
        ],
        compiler_params=pltpu.CompilerParams(vmem_limit_bytes=32 * MIB),
        cost_estimate=pl.CostEstimate(flops=1, bytes_accessed=1, transcendentals=0),
        name="project",
    )(*operands, *weights)


def finish_kernel(kept, received, *rest):
    rest[-1][...] = (kept[...] + received[...].astype(jnp.float32)).astype(jnp.bfloat16)


def finish(kept, received, first, out):
    columns, start = received.shape[1], first // TILE
    tile = pl.BlockSpec((BLOCK, TILE), lambda j: (0, start + j))
    in_specs = [tile, pl.BlockSpec((BLOCK, TILE), lambda j: (0, j))]
    operands = [kept, received]
    if out is not None:
        in_specs.append(pl.BlockSpec(memory_space=pl.ANY))
        operands.append(out)
    return pl.pallas_call(
        finish_kernel,
        out_shape=jax.ShapeDtypeStruct(kept.shape, jnp.bfloat16),
        grid=(columns // TILE,),
        in_specs=in_specs,
        out_specs=tile,
        input_output_aliases={} if out is None else {2: 0},
        compiler_params=pltpu.CompilerParams(vmem_limit_bytes=32 * MIB),
        cost_estimate=pl.CostEstimate(
            flops=BLOCK * columns, bytes_accessed=8 * BLOCK * columns, transcendentals=0
        ),
        name="finish",
    )(*operands)


def body(queries, key_heads, value_heads, doc_lengths, out_weight):
    s = lax.axis_index("seq")
    t = lax.axis_index("tensor")
    hi, core = t // 2, t % 2

    query_pos = s * BLOCK + jnp.arange(BLOCK, dtype=jnp.int32)
    cosine, sine = rope_tables(query_pos)
    own_key = lax.dynamic_index_in_dim(key_heads, hi, 1, keepdims=False).astype(jnp.float32)
    own_key = rope(own_key, cosine, sine).astype(jnp.bfloat16)
    own_value = lax.dynamic_index_in_dim(value_heads, hi, 1, keepdims=False)
    block = jnp.concatenate([own_key, own_value], axis=1)

    q_own = turn(queries, cosine, sine)
    q_other = permute(q_own, other_core)
    near = [permute(block, along_rows(step)) for step in (1, 2)]
    far = permute(block, far_block)
    half = lax.dynamic_slice_in_dim(block, core * (BLOCK // 2), BLOCK // 2, 0)
    group_1 = jnp.concatenate([half, *near], axis=0)
    near = jnp.concatenate(near, axis=0)
    group_1, near, q_other, far, out_weight = lax.optimization_barrier(
        (group_1, near, q_other, far, out_weight)
    )
    other_weight = permute(out_weight, other_core)
    shifts = (1, -1, 2)
    group_2 = permute(near, two_rows_on)
    columns_1 = [permute(group_1, in_row(shift)) for shift in shifts]

    q_all = jnp.concatenate([q_own, q_other], axis=1)
    doc_ends = jnp.cumsum(doc_lengths)
    low = jnp.max(jnp.where(doc_ends[:, None] <= query_pos[None], doc_ends[:, None], 0), axis=0)
    low = jnp.broadcast_to(low, (8, HEADS, BLOCK)).reshape(8, LANES)
    step = functools.partial(attend, q_all, low)

    state = step([half, near], [("half", 0), (1, 0), (2, 0)])
    rows_2 = lambda shift: [(3, shift), (4, shift)]
    columns_2 = []
    for shift, keys in zip(shifts, columns_1):
        group_2, state = lax.optimization_barrier((group_2, state))
        columns_2.append(permute(group_2, in_row(shift)))
        refs, kinds = [keys], [("half", shift), (1, shift), (2, shift)]
        if shift == 1:
            refs, kinds = [group_2] + refs, rows_2(0) + kinds
        if shift == 2:
            refs, kinds = refs + [far], kinds + [("far", 0)]
        state = step(refs, kinds, state)
    state, other_weight = lax.optimization_barrier((state, other_weight))
    weights = (out_weight, other_weight)
    state = step(columns_2[:2], rows_2(1) + rows_2(-1), state)
    state = step(columns_2[2:], rows_2(2), state)

    theirs = permute(state, other_core)
    attended, partial = project((state, theirs), weights, True, 0, (512,), jnp.bfloat16, True)
    received = [permute(partial, other_hi)]
    for partial in project((attended,), weights, True, 512, (512,) * 3, jnp.bfloat16):
        received.append(permute(partial, other_hi))
    (kept,) = project((attended,), weights, False, 0, (OUT_COLUMNS,), jnp.float32)
    out, first = None, 0
    for piece in received:
        out = finish(kept, piece, first, out)
        first += piece.shape[1]
    return out


def solution(mesh):
    return jax.shard_map(
        body,
        mesh=mesh,
        in_specs=(
            P("seq", "tensor"),
            P("seq", None, None),
            P("seq", None, None),
            P(),
            P("tensor", None),
        ),
        out_specs=P("seq", "tensor"),
        check_vma=False,
    )
```

profile of v0, /device:TPU:6, one launch (start us, length us, event | category | flops | bytes accessed | tf_op | source)
XLA Modules:
  0.0 92.1 jit_solution(9096977632570388984)
XLA Ops:
  0.1 1.3 %constant_dynamic-slice_fusion.1 = (bf16[256,1,128]{2,1,0:T(2,128)(2,1)S(1)}, bf16[256,1,128]{2,1,0:T(2,128)(2,1)S(1)}) fusion(bf16[256,2,128]{2,1,0:T(2,128)(2,1)} %param.7, s32[]{:T(128)S(6)} %select_n.24, bf16[256,2,128]{2,1,0:T(2,128)(2,1)} %param.6), kind=kLoop, calls=%fused_computation.15 | loop fusion | bytes 262148 | tf_op jit(solution)/shard_map/jit(dynamic_index_in_dim)/dynamic_slice | solution.py:310
  1.4 0.6 subtract_convert_fusion
  2.0 0.1 pad_maximum_fusion.3
  2.1 0.0 copy-start.1
  2.1 5.2 %collective-permute-start.1 = (bf16[256,256]{1,0:T(8,128)(2,1)S(1)}, bf16[256,256]{1,0:T(8,128)(2,1)S(1)}, u32[]{:S(2)}, u32[]{:S(2)}) collective-permute-start(bf16[256,256]{1,0:T(8,128)(2,1)S(1)} %pad_maximum_fusion.3), channel_id=1, source_target_pairs={{0,32},{1,113},{2,34},{3,115},{4,36},{5,117},{6,38},{7,119},{8,40}... | collective-permute-start | bytes 393224 | tf_op jit(solution)/shard_map/ppermute | solution.py:44
  7.3 3.8 %collective-permute-start = (bf16[256,256]{1,0:T(8,128)(2,1)S(1)}, bf16[256,256]{1,0:T(8,128)(2,1)S(1)}, u32[]{:S(2)}, u32[]{:S(2)}) collective-permute-start(bf16[256,256]{1,0:T(8,128)(2,1)S(1)} %pad_maximum_fusion.3), channel_id=1, source_target_pairs={{0,16},{1,129},{2,18},{3,131},{4,20},{5,133},{6,22},{7,135},{8,24}... | collective-permute-start | bytes 393224 | tf_op jit(solution)/shard_map/ppermute | solution.py:44
  11.1 0.7 collective-permute-start.3
  11.8 1.0 %turn.1 = bf16[128,1024]{1,0:T(8,128)(2,1)S(1)} custom-call(bf16[256,512]{1,0:T(8,128)(2,1)S(1)} %copy-done, f32[256,64]{1,0:T(8,128)S(1)} %get-tuple-element.44.cosine, f32[256,64]{1,0:T(8,128)S(1)} %get-tuple-element.43.sine), custom_call_target="tpu_custom_call" | custom-call | flops 1 | bytes 1 | tf_op jit(solution)/shard_map/turn/pallas_call | solution.py:196
  12.8 0.9 collective-permute-start.2
  13.7 2.7 %collective-permute-done = bf16[256,256]{1,0:T(8,128)(2,1)S(1)} collective-permute-done((bf16[256,256]{1,0:T(8,128)(2,1)S(1)}, bf16[256,256]{1,0:T(8,128)(2,1)S(1)}, u32[]{:S(2)}, u32[]{:S(2)}) %collective-permute-start) | collective-permute-done | bytes 131104 | tf_op jit(solution)/shard_map/ppermute | solution.py:44
  16.4 0.0 collective-permute-done.3.rest_1_
  16.4 0.0 collective-permute-done.2
  16.4 0.3 collective-permute-start.11
  16.7 0.2 reduce-window.8
  16.9 0.1 select_reduce_fusion
  17.0 3.1 %collective-permute-start.6 = (bf16[640,256]{1,0:T(8,128)(2,1)S(1)}, bf16[640,256]{1,0:T(8,128)(2,1)S(1)}, u32[]{:S(2)}, u32[]{:S(2)}) collective-permute-start(bf16[640,256]{1,0:T(8,128)(2,1)S(1)} %pad_maximum_fusion.1), channel_id=1, source_target_pairs={{0,12},{1,13},{2,14},{3,15},{4,0},{5,1},{6,2},{7,3},{8,4},{9,5},{1... | collective-permute-start | bytes 983048 | tf_op jit(solution)/shard_map/ppermute | solution.py:44
  20.0 8.8 %collective-permute-start.4 = (bf16[512,256]{1,0:T(8,128)(2,1)S(1)}, bf16[512,256]{1,0:T(8,128)(2,1)S(1)}, u32[]{:S(2)}, u32[]{:S(2)}) collective-permute-start(bf16[512,256]{1,0:T(8,128)(2,1)S(1)} %pad_maximum_fusion.2.rest_1_), channel_id=1, source_target_pairs={{0,32},{1,225},{2,34},{3,227},{4,36},{5,229},{6,38},{7,231},{8,40}... | collective-permute-start | bytes 786440 | tf_op jit(solution)/shard_map/ppermute | solution.py:44
  28.8 0.1 collective-permute-start.10
  29.0 2.2 %attend.6.rest_2_ = f32[136,2048]{1,0:T(8,128)S(1)} custom-call(bf16[128,2048]{1,0:T(8,128)(2,1)S(1)} %pad_maximum_fusion.q_ref, s32[8,2048]{1,0:T(8,128)S(1)} %broadcast_in_dim.25.low_ref, bf16[128,256]{1,0:T(8,128)(2,1)S(1)} %constant_dynamic-slice_fusion.rest_0_, bf16[512,256]{1,0:T(8,128)(2,1)S(1)} %pad_maximum_fusion.2.rest_1_), custom_call_target="tpu_custom_call" | custom-call | flops 1 | bytes 1 | tf_op jit(solution)/shard_map/attend/pallas_call | solution.py:175
  31.2 1.8 %collective-permute-done.4.rest_0_ = bf16[512,256]{1,0:T(8,128)(2,1)S(1)} collective-permute-done((bf16[512,256]{1,0:T(8,128)(2,1)S(1)}, bf16[512,256]{1,0:T(8,128)(2,1)S(1)}, u32[]{:S(2)}, u32[]{:S(2)}) %collective-permute-start.4) | collective-permute-done | bytes 262176 | tf_op jit(solution)/shard_map/ppermute | solution.py:44
  33.1 0.7 collective-permute-start.8
  33.8 4.2 %collective-permute-done.5.rest_1_ = bf16[640,256]{1,0:T(8,128)(2,1)S(1)} collective-permute-done((bf16[640,256]{1,0:T(8,128)(2,1)S(1)}, bf16[640,256]{1,0:T(8,128)(2,1)S(1)}, u32[]{:S(2)}, u32[]{:S(2)}) %collective-permute-start.5) | collective-permute-done | bytes 327712 | tf_op jit(solution)/shard_map/ppermute | solution.py:44
  37.9 4.3 %attend.7.rest_1_ = f32[136,2048]{1,0:T(8,128)S(1)} custom-call(bf16[128,2048]{1,0:T(8,128)(2,1)S(1)} %pad_maximum_fusion.q_ref, s32[8,2048]{1,0:T(8,128)S(1)} %broadcast_in_dim.25.low_ref, bf16[512,256]{1,0:T(8,128)(2,1)S(1)} %collective-permute-done.4.rest_0_, bf16[640,256]{1,0:T(8,128)(2,1)S(1)} %collective-permute-done.5.rest_1_, ...), custom_call_target="tpu_custom_call", output_to_operand_aliasing={{}: (4, {})} | custom-call | flops 1 | bytes 1 | tf_op jit(solution)/shard_map/attend/pallas_call | solution.py:175
  42.3 0.1 collective-permute-start.9
  42.3 0.0 collective-permute-done.6.rest_0_
  42.4 2.5 %attend.8.rest_2_ = f32[136,2048]{1,0:T(8,128)S(1)} custom-call(bf16[128,2048]{1,0:T(8,128)(2,1)S(1)} %pad_maximum_fusion.q_ref, s32[8,2048]{1,0:T(8,128)S(1)} %broadcast_in_dim.25.low_ref, bf16[640,256]{1,0:T(8,128)(2,1)S(1)} %collective-permute-done.6.rest_0_, f32[136,2048]{1,0:T(8,128)S(1)} %attend.7.rest_1_), custom_call_target="tpu_custom_call", output_to_operand_aliasing={{}: (3, {})} | custom-call | flops 1 | bytes 1 | tf_op jit(solution)/shard_map/attend/pallas_call | solution.py:175
  44.9 0.0 slice-start.1
  44.9 0.1 collective-permute-start.7
  45.0 3.2 %attend.9.rest_2_ = f32[136,2048]{1,0:T(8,128)S(1)} custom-call(bf16[128,2048]{1,0:T(8,128)(2,1)S(1)} %pad_maximum_fusion.q_ref, s32[8,2048]{1,0:T(8,128)S(1)} %broadcast_in_dim.25.low_ref, bf16[640,256]{1,0:T(8,128)(2,1)S(1)} %collective-permute-done.10.rest_0_, ...), custom_call_target="tpu_custom_call", output_to_operand_aliasing={{}: (4, {})} | custom-call | flops 1 | bytes 1 | tf_op jit(solution)/shard_map/attend/pallas_call | solution.py:175
  48.2 5.9 %collective-permute-done.9.rest_1_ = bf16[512,256]{1,0:T(8,128)(2,1)S(1)} collective-permute-done((bf16[512,256]{1,0:T(8,128)(2,1)S(1)}, bf16[512,256]{1,0:T(8,128)(2,1)S(1)}, u32[]{:S(2)}, u32[]{:S(2)}) %collective-permute-start.9) | collective-permute-done | bytes 262176 | tf_op jit(solution)/shard_map/ppermute | solution.py:44
  54.1 3.9 %attend.10.rest_1_ = f32[136,2048]{1,0:T(8,128)S(1)} custom-call(bf16[128,2048]{1,0:T(8,128)(2,1)S(1)} %pad_maximum_fusion.q_ref, s32[8,2048]{1,0:T(8,128)S(1)} %broadcast_in_dim.25.low_ref, bf16[512,256]{1,0:T(8,128)(2,1)S(1)} %collective-permute-done.8.rest_0_, ...), custom_call_target="tpu_custom_call", output_to_operand_aliasing={{}: (4, {})} | custom-call | flops 1 | bytes 1 | tf_op jit(solution)/shard_map/attend/pallas_call | solution.py:175
  58.0 2.1 %attend.11.rest_0_ = f32[136,2048]{1,0:T(8,128)S(1)} custom-call(bf16[128,2048]{1,0:T(8,128)(2,1)S(1)} %pad_maximum_fusion.q_ref, s32[8,2048]{1,0:T(8,128)S(1)} %broadcast_in_dim.25.low_ref, bf16[512,256]{1,0:T(8,128)(2,1)S(1)} %collective-permute-done.7.rest_0_, f32[136,2048]{1,0:T(8,128)S(1)} %attend.10.rest_1_), custom_call_target="tpu_custom_call", output_to_operand_aliasing={{}: (3, {})} | custom-call | flops 1 | bytes 1 | tf_op jit(solution)/shard_map/attend/pallas_call | solution.py:175
  60.1 0.1 collective-permute-start.12
  60.2 2.7 %collective-permute-done.12.rest_1_ = f32[136,2048]{1,0:T(8,128)S(1)} collective-permute-done((f32[136,2048]{1,0:T(8,128)S(1)}, f32[136,2048]{1,0:T(8,128)S(1)}, u32[]{:S(2)}, u32[]{:S(2)}) %collective-permute-start.12) | collective-permute-done | bytes 1114144 | tf_op jit(solution)/shard_map/ppermute | solution.py:44
  62.9 1.7 %project.3 = (bf16[256,1024]{1,0:T(8,128)(2,1)S(1)}, bf16[256,512]{1,0:T(8,128)(2,1)S(1)}) custom-call(f32[136,2048]{1,0:T(8,128)S(1)} %attend.11.rest_0_, f32[136,2048]{1,0:T(8,128)S(1)} %collective-permute-done.12.rest_1_, bf16[512,8192]{1,0:T(8,128)(2,1)S(1)} %bitcast.14, bf16[512,8192]{1,0:T(8,128)(2,1)} %collective-permute-done.11.rest_3_.rest_2_), custom_call_target="tpu_custom_call" | custom-call | flops 1 | bytes 1 | tf_op jit(solution)/shard_map/project/pallas_call | solution.py:258
  64.6 1.5 %collective-permute-start.16 = (bf16[256,512]{1,0:T(8,128)(2,1)S(1)}, bf16[256,512]{1,0:T(8,128)(2,1)S(1)}, u32[]{:S(2)}, u32[]{:S(2)}) collective-permute-start(bf16[256,512]{1,0:T(8,128)(2,1)S(1)} %get-tuple-element.40), channel_id=1, source_target_pairs={{0,2},{1,3},{2,0},{3,1},{4,6},{5,7},{6,4},{7,5},{8,10},{9,11},{10,... | collective-permute-start | bytes 786440 | tf_op jit(solution)/shard_map/ppermute | solution.py:44
  66.1 2.5 %project.5 = (bf16[256,512]{1,0:T(8,128)(2,1)S(1)}, bf16[256,512]{1,0:T(8,128)(2,1)S(1)}, bf16[256,512]{1,0:T(8,128)(2,1)S(1)}) custom-call(bf16[256,1024]{1,0:T(8,128)(2,1)S(1)} %get-tuple-element.36.rest_0_, bf16[512,8192]{1,0:T(8,128)(2,1)S(1)} %bitcast.14, bf16[512,8192]{1,0:T(8,128)(2,1)} %collective-permute-done.11.rest_3_.rest_2_), custom_call_target="tpu_custom_call" | custom-call | flops 1 | bytes 1 | tf_op jit(solution)/shard_map/project/pallas_call | solution.py:258
  68.6 2.2 %collective-permute-start.15 = (bf16[256,512]{1,0:T(8,128)(2,1)S(1)}, bf16[256,512]{1,0:T(8,128)(2,1)S(1)}, u32[]{:S(2)}, u32[]{:S(2)}) collective-permute-start(bf16[256,512]{1,0:T(8,128)(2,1)S(1)} %get-tuple-element.39), channel_id=1, source_target_pairs={{0,2},{1,3},{2,0},{3,1},{4,6},{5,7},{6,4},{7,5},{8,10},{9,11},{10,... | collective-permute-start | bytes 786440 | tf_op jit(solution)/shard_map/ppermute | solution.py:44
  70.8 1.4 %collective-permute-start.14 = (bf16[256,512]{1,0:T(8,128)(2,1)S(1)}, bf16[256,512]{1,0:T(8,128)(2,1)S(1)}, u32[]{:S(2)}, u32[]{:S(2)}) collective-permute-start(bf16[256,512]{1,0:T(8,128)(2,1)S(1)} %get-tuple-element.38), channel_id=1, source_target_pairs={{0,2},{1,3},{2,0},{3,1},{4,6},{5,7},{6,4},{7,5},{8,10},{9,11},{10,... | collective-permute-start | bytes 786440 | tf_op jit(solution)/shard_map/ppermute | solution.py:44
  72.2 2.1 %collective-permute-start.13 = (bf16[256,512]{1,0:T(8,128)(2,1)S(1)}, bf16[256,512]{1,0:T(8,128)(2,1)S(1)}, u32[]{:S(2)}, u32[]{:S(2)}) collective-permute-start(bf16[256,512]{1,0:T(8,128)(2,1)S(1)} %get-tuple-element.37), channel_id=1, source_target_pairs={{0,2},{1,3},{2,0},{3,1},{4,6},{5,7},{6,4},{7,5},{8,10},{9,11},{10,... | collective-permute-start | bytes 786440 | tf_op jit(solution)/shard_map/ppermute | solution.py:44
  74.3 2.9 %project.4.kept = f32[256,2048]{1,0:T(8,128)S(1)} custom-call(bf16[256,1024]{1,0:T(8,128)(2,1)S(1)} %get-tuple-element.36.rest_0_, bf16[512,8192]{1,0:T(8,128)(2,1)S(1)} %bitcast.14, bf16[512,8192]{1,0:T(8,128)(2,1)} %collective-permute-done.11.rest_3_.rest_2_), custom_call_target="tpu_custom_call" | custom-call | flops 1 | bytes 1 | tf_op jit(solution)/shard_map/project/pallas_call | solution.py:258
  77.3 0.7 finish.4.rest_0_
  78.1 2.9 %collective-permute-done.15.received = bf16[256,512]{1,0:T(8,128)(2,1)S(1)} collective-permute-done((bf16[256,512]{1,0:T(8,128)(2,1)S(1)}, bf16[256,512]{1,0:T(8,128)(2,1)S(1)}, u32[]{:S(2)}, u32[]{:S(2)}) %collective-permute-start.15) | collective-permute-done | bytes 262176 | tf_op jit(solution)/shard_map/ppermute | solution.py:44
  81.0 0.7 finish.5.rest_0_
  81.7 4.9 %collective-permute-done.14.received = bf16[256,512]{1,0:T(8,128)(2,1)S(1)} collective-permute-done((bf16[256,512]{1,0:T(8,128)(2,1)S(1)}, bf16[256,512]{1,0:T(8,128)(2,1)S(1)}, u32[]{:S(2)}, u32[]{:S(2)}) %collective-permute-start.14) | collective-permute-done | bytes 262176 | tf_op jit(solution)/shard_map/ppermute | solution.py:44
  86.6 0.7 finish.6.rest_0_
  87.3 4.1 %collective-permute-done.13.received = bf16[256,512]{1,0:T(8,128)(2,1)S(1)} collective-permute-done((bf16[256,512]{1,0:T(8,128)(2,1)S(1)}, bf16[256,512]{1,0:T(8,128)(2,1)S(1)}, u32[]{:S(2)}, u32[]{:S(2)}) %collective-permute-start.13) | collective-permute-done | bytes 262176 | tf_op jit(solution)/shard_map/ppermute | solution.py:44
  91.4 0.7 finish.7
  (25 shorter events, 0.2 us)
Async XLA Ops:
  0.0 11.8 %copy-start = (bf16[256,512]{1,0:T(8,128)(2,1)S(1)}, bf16[256,512]{1,0:T(8,128)(2,1)}, u32[]{:S(2)}) copy-start(bf16[256,512]{1,0:T(8,128)(2,1)} %queries.1) | copy-start | bytes 786436
  2.1 14.6 %copy-start.1 = (s32[8]{0:T(128)S(1)}, s32[8]{0:T(128)}, u32[]{:S(2)}) copy-start(s32[8]{0:T(128)} %param.8) | copy-start | bytes 100
  2.1 11.6 %collective-permute-start.1 = (bf16[256,256]{1,0:T(8,128)(2,1)S(1)}, bf16[256,256]{1,0:T(8,128)(2,1)S(1)}, u32[]{:S(2)}, u32[]{:S(2)}) collective-permute-start(bf16[256,256]{1,0:T(8,128)(2,1)S(1)} %pad_maximum_fusion.3), channel_id=1, source_target_pairs={{0,32},{1,113},{2,34},{3,115},{4,36},{5,117},{6,38},{7,119},{8,40}... | collective-permute-start | bytes 393224 | tf_op jit(solution)/shard_map/ppermute | solution.py:44
  7.3 9.1 %collective-permute-start = (bf16[256,256]{1,0:T(8,128)(2,1)S(1)}, bf16[256,256]{1,0:T(8,128)(2,1)S(1)}, u32[]{:S(2)}, u32[]{:S(2)}) collective-permute-start(bf16[256,256]{1,0:T(8,128)(2,1)S(1)} %pad_maximum_fusion.3), channel_id=1, source_target_pairs={{0,16},{1,129},{2,18},{3,131},{4,20},{5,133},{6,22},{7,135},{8,24}... | collective-permute-start | bytes 393224 | tf_op jit(solution)/shard_map/ppermute | solution.py:44
  11.1 5.3 %collective-permute-start.3 = (bf16[256,256]{1,0:T(8,128)(2,1)S(1)}, bf16[256,256]{1,0:T(8,128)(2,1)S(1)}, u32[]{:S(2)}, u32[]{:S(2)}) collective-permute-start(bf16[256,256]{1,0:T(8,128)(2,1)S(1)} %pad_maximum_fusion.3), channel_id=1, source_target_pairs={{12,144},{14,146},{28,160},{30,162},{44,176},{46,178},{60,192},{62... | collective-permute-start | bytes 393224 | tf_op jit(solution)/shard_map/ppermute | solution.py:44
  12.8 3.6 %collective-permute-start.2 = (bf16[128,1024]{1,0:T(8,128)(2,1)S(1)}, bf16[128,1024]{1,0:T(8,128)(2,1)S(1)}, u32[]{:S(2)}, u32[]{:S(2)}) collective-permute-start(bf16[128,1024]{1,0:T(8,128)(2,1)S(1)} %turn.1), channel_id=1, source_target_pairs={{0,1},{1,0},{2,3},{3,2},{4,5},{5,4},{6,7},{7,6},{8,9},{9,8},{10,11... | collective-permute-start | bytes 786440 | tf_op jit(solution)/shard_map/ppermute | solution.py:44
  16.4 31.8 %collective-permute-start.11 = (bf16[512,8192]{1,0:T(8,128)(2,1)}, bf16[512,8192]{1,0:T(8,128)(2,1)}, u32[]{:S(2)}, u32[]{:S(2)}) collective-permute-start(bf16[512,8192]{1,0:T(8,128)(2,1)} %rest_1_.1), channel_id=1, source_target_pairs={{0,1},{1,0},{2,3},{3,2},{4,5},{5,4},{6,7},{7,6},{8,9},{9,8},{10,11... | collective-permute-start | bytes 25165832 | tf_op jit(solution)/shard_map/ppermute | solution.py:44
  17.0 25.4 %collective-permute-start.6 = (bf16[640,256]{1,0:T(8,128)(2,1)S(1)}, bf16[640,256]{1,0:T(8,128)(2,1)S(1)}, u32[]{:S(2)}, u32[]{:S(2)}) collective-permute-start(bf16[640,256]{1,0:T(8,128)(2,1)S(1)} %pad_maximum_fusion.1), channel_id=1, source_target_pairs={{0,12},{1,13},{2,14},{3,15},{4,0},{5,1},{6,2},{7,3},{8,4},{9,5},{1... | collective-permute-start | bytes 983048 | tf_op jit(solution)/shard_map/ppermute | solution.py:44
  20.0 17.9 %collective-permute-start.5 = (bf16[640,256]{1,0:T(8,128)(2,1)S(1)}, bf16[640,256]{1,0:T(8,128)(2,1)S(1)}, u32[]{:S(2)}, u32[]{:S(2)}) collective-permute-start(bf16[640,256]{1,0:T(8,128)(2,1)S(1)} %pad_maximum_fusion.1), channel_id=1, source_target_pairs={{0,4},{1,5},{2,6},{3,7},{4,8},{5,9},{6,10},{7,11},{8,12},{9,13},{1... | collective-permute-start | bytes 983048 | tf_op jit(solution)/shard_map/ppermute | solution.py:44
  20.0 13.1 %collective-permute-start.4 = (bf16[512,256]{1,0:T(8,128)(2,1)S(1)}, bf16[512,256]{1,0:T(8,128)(2,1)S(1)}, u32[]{:S(2)}, u32[]{:S(2)}) collective-permute-start(bf16[512,256]{1,0:T(8,128)(2,1)S(1)} %pad_maximum_fusion.2.rest_1_), channel_id=1, source_target_pairs={{0,32},{1,225},{2,34},{3,227},{4,36},{5,229},{6,38},{7,231},{8,40}... | collective-permute-start | bytes 786440 | tf_op jit(solution)/shard_map/ppermute | solution.py:44
  28.8 16.1 %collective-permute-start.10 = (bf16[640,256]{1,0:T(8,128)(2,1)S(1)}, bf16[640,256]{1,0:T(8,128)(2,1)S(1)}, u32[]{:S(2)}, u32[]{:S(2)}) collective-permute-start(bf16[640,256]{1,0:T(8,128)(2,1)S(1)} %pad_maximum_fusion.1), channel_id=1, source_target_pairs={{0,8},{1,9},{2,10},{3,11},{4,12},{5,13},{6,14},{7,15},{8,0},{9,1},... | collective-permute-start | bytes 983048 | tf_op jit(solution)/shard_map/ppermute | solution.py:44
  33.1 15.1 %collective-permute-start.8 = (bf16[512,256]{1,0:T(8,128)(2,1)S(1)}, bf16[512,256]{1,0:T(8,128)(2,1)S(1)}, u32[]{:S(2)}, u32[]{:S(2)}) collective-permute-start(bf16[512,256]{1,0:T(8,128)(2,1)S(1)} %collective-permute-done.4.rest_0_), channel_id=1, source_target_pairs={{0,4},{1,5},{2,6},{3,7},{4,8},{5,9},{6,10},{7,11},{8,12},{9,13},{1... | collective-permute-start | bytes 786440 | tf_op jit(solution)/shard_map/ppermute | solution.py:44
  37.9 25.0 %slice-start = ((s8[8388608]{0:T(1024)(128)(4,1)}), s8[4194304]{0:T(1024)(128)(4,1)S(1)}, s32[]{:S(2)}) async-start(s8[8388608]{0:T(1024)(128)(4,1)} %bitcast.13), calls=%async_computation | async-start | bytes 8388608
  42.3 11.9 %collective-permute-start.9 = (bf16[512,256]{1,0:T(8,128)(2,1)S(1)}, bf16[512,256]{1,0:T(8,128)(2,1)S(1)}, u32[]{:S(2)}, u32[]{:S(2)}) collective-permute-start(bf16[512,256]{1,0:T(8,128)(2,1)S(1)} %collective-permute-done.4.rest_0_), channel_id=1, source_target_pairs={{0,12},{1,13},{2,14},{3,15},{4,0},{5,1},{6,2},{7,3},{8,4},{9,5},{1... | collective-permute-start | bytes 786440 | tf_op jit(solution)/shard_map/ppermute | solution.py:44
  44.9 18.1 %slice-start.1 = ((s8[8388608]{0:T(1024)(128)(4,1)}), s8[4194304]{0:T(1024)(128)(4,1)S(1)}, s32[]{:S(2)}) async-start(s8[8388608]{0:T(1024)(128)(4,1)} %bitcast.13), calls=%async_computation.1 | async-start | bytes 8388608
  44.9 13.1 %collective-permute-start.7 = (bf16[512,256]{1,0:T(8,128)(2,1)S(1)}, bf16[512,256]{1,0:T(8,128)(2,1)S(1)}, u32[]{:S(2)}, u32[]{:S(2)}) collective-permute-start(bf16[512,256]{1,0:T(8,128)(2,1)S(1)} %collective-permute-done.4.rest_0_), channel_id=1, source_target_pairs={{0,8},{1,9},{2,10},{3,11},{4,12},{5,13},{6,14},{7,15},{8,0},{9,1},... | collective-permute-start | bytes 786440 | tf_op jit(solution)/shard_map/ppermute | solution.py:44
  60.1 2.8 %collective-permute-start.12 = (f32[136,2048]{1,0:T(8,128)S(1)}, f32[136,2048]{1,0:T(8,128)S(1)}, u32[]{:S(2)}, u32[]{:S(2)}) collective-permute-start(f32[136,2048]{1,0:T(8,128)S(1)} %attend.11.rest_0_), channel_id=1, source_target_pairs={{0,1},{1,0},{2,3},{3,2},{4,5},{5,4},{6,7},{7,6},{8,9},{9,8},{10,11... | collective-permute-start | bytes 3342344 | tf_op jit(solution)/shard_map/ppermute | solution.py:44
  64.6 12.7 %collective-permute-start.16 = (bf16[256,512]{1,0:T(8,128)(2,1)S(1)}, bf16[256,512]{1,0:T(8,128)(2,1)S(1)}, u32[]{:S(2)}, u32[]{:S(2)}) collective-permute-start(bf16[256,512]{1,0:T(8,128)(2,1)S(1)} %get-tuple-element.40), channel_id=1, source_target_pairs={{0,2},{1,3},{2,0},{3,1},{4,6},{5,7},{6,4},{7,5},{8,10},{9,11},{10,... | collective-permute-start | bytes 786440 | tf_op jit(solution)/shard_map/ppermute | solution.py:44
  68.6 12.4 %collective-permute-start.15 = (bf16[256,512]{1,0:T(8,128)(2,1)S(1)}, bf16[256,512]{1,0:T(8,128)(2,1)S(1)}, u32[]{:S(2)}, u32[]{:S(2)}) collective-permute-start(bf16[256,512]{1,0:T(8,128)(2,1)S(1)} %get-tuple-element.39), channel_id=1, source_target_pairs={{0,2},{1,3},{2,0},{3,1},{4,6},{5,7},{6,4},{7,5},{8,10},{9,11},{10,... | collective-permute-start | bytes 786440 | tf_op jit(solution)/shard_map/ppermute | solution.py:44
  70.8 15.8 %collective-permute-start.14 = (bf16[256,512]{1,0:T(8,128)(2,1)S(1)}, bf16[256,512]{1,0:T(8,128)(2,1)S(1)}, u32[]{:S(2)}, u32[]{:S(2)}) collective-permute-start(bf16[256,512]{1,0:T(8,128)(2,1)S(1)} %get-tuple-element.38), channel_id=1, source_target_pairs={{0,2},{1,3},{2,0},{3,1},{4,6},{5,7},{6,4},{7,5},{8,10},{9,11},{10,... | collective-permute-start | bytes 786440 | tf_op jit(solution)/shard_map/ppermute | solution.py:44
  72.2 19.2 %collective-permute-start.13 = (bf16[256,512]{1,0:T(8,128)(2,1)S(1)}, bf16[256,512]{1,0:T(8,128)(2,1)S(1)}, u32[]{:S(2)}, u32[]{:S(2)}) collective-permute-start(bf16[256,512]{1,0:T(8,128)(2,1)S(1)} %get-tuple-element.37), channel_id=1, source_target_pairs={{0,2},{1,3},{2,0},{3,1},{4,6},{5,7},{6,4},{7,5},{8,10},{9,11},{10,... | collective-permute-start | bytes 786440 | tf_op jit(solution)/shard_map/ppermute | solution.py:44
where the time goes:
time: 92 us; the launch traced here: 92.1 us
  starting transfers between devices  30.9 us (34%)
  Pallas kernels  29.3 us (32%)
  waiting for transfers between devices  29.2 us (32%)
  local copies, waits for them, and re-layouts  1.33 us (1%)
  other arithmetic  1.06 us (1%)
    ppermute x17, starting transfers between devices, permute(): return lax.ppermute(x, ('seq', 'tensor'), device_perm(move))  30.9 us
    ppermute x17, waiting for transfers between devices, permute(): return lax.ppermute(x, ('seq', 'tensor'), device_perm(move))  29.2 us
    pallas_call x6, Pallas kernels, attend(): pl.pallas_call(functools.partial(attend_kernel, kinds, state is None), ou...  18.2 us
    pallas_call x3, Pallas kernels, project(): pl.pallas_call(functools.partial(project_kernel, other_side, first, mergi...  7.1 us
    pallas_call x4, Pallas kernels, finish(): pl.pallas_call(finish_kernel, out_shape=jax.ShapeDtypeStruct(kept.shape,...  2.99 us
  transfers between devices with their start and end apart: 17, of which 8 were waited for; matrix products, arithmetic and copies ran while one was open for 0% of the time, Pallas kernels for 27%

commit v1 on v0

--- a/solution.py
+++ b/solution.py
@@ -314,11 +314,12 @@
     q_other = permute(q_own, other_core)
     near = [permute(block, along_rows(step)) for step in (1, 2)]
     far = permute(block, far_block)
+    *near, far = lax.optimization_barrier((*near, far))
     half = lax.dynamic_slice_in_dim(block, core * (BLOCK // 2), BLOCK // 2, 0)
     group_1 = jnp.concatenate([half, *near], axis=0)
     near = jnp.concatenate(near, axis=0)
-    group_1, near, q_other, far, out_weight = lax.optimization_barrier(
-        (group_1, near, q_other, far, out_weight)
+    group_1, near, q_other, out_weight = lax.optimization_barrier(
+        (group_1, near, q_other, out_weight)
     )
     other_weight = permute(out_weight, other_core)
     shifts = (1, -1, 2)
@@ -333,10 +334,9 @@
 
     state = step([half, near], [("half", 0), (1, 0), (2, 0)])
     rows_2 = lambda shift: [(3, shift), (4, shift)]
-    columns_2 = []
+    group_2, state = lax.optimization_barrier((group_2, state))
+    columns_2 = [permute(group_2, in_row(shift)) for shift in shifts]
     for shift, keys in zip(shifts, columns_1):
-        group_2, state = lax.optimization_barrier((group_2, state))
-        columns_2.append(permute(group_2, in_row(shift)))
         refs, kinds = [keys], [("half", shift), (1, shift), (2, shift)]
         if shift == 1:
             refs, kinds = [group_2] + refs, rows_2(0) + kinds

time: 92 us -> 88.7 us (0.964)
  waiting for transfers between devices: 29.2 us -> 26.1 us
    ppermute x17, waiting for transfers between devices: 29.2 us -> 26.1 us  [permute(): return lax.ppermute(x, ('seq', 'tensor'), device_perm(move))]
  transfers between devices with their start and end apart: 17 -> 17, of which waited for: 8 -> 8; matrix products, arithmetic and copies ran while one was open for 0% -> 0% of each run, Pallas kernels for 27% -> 28%
where the time goes in v1:
time: 88.7 us; the launch traced here: 88.4 us
  starting transfers between devices  30.4 us (34%)
  Pallas kernels  29.3 us (33%)
  waiting for transfers between devices  26.1 us (29%)
  local copies, waits for them, and re-layouts  1.33 us (1%)
  other arithmetic  1.06 us (1%)
    ppermute x17, starting transfers between devices, permute(): return lax.ppermute(x, ('seq', 'tensor'), device_perm(move))  30.4 us
    ppermute x17, waiting for transfers between devices, permute(): return lax.ppermute(x, ('seq', 'tensor'), device_perm(move))  26.1 us
    pallas_call x6, Pallas kernels, attend(): pl.pallas_call(functools.partial(attend_kernel, kinds, state is None), ou...  18.2 us
    pallas_call x3, Pallas kernels, project(): pl.pallas_call(functools.partial(project_kernel, other_side, first, mergi...  7.1 us
    pallas_call x4, Pallas kernels, finish(): pl.pallas_call(finish_kernel, out_shape=jax.ShapeDtypeStruct(kept.shape,...  2.99 us
  transfers between devices with their start and end apart: 17, of which 8 were waited for; matrix products, arithmetic and copies ran while one was open for 0% of the time, Pallas kernels for 28%

profile of v1, /device:TPU:6, one launch (start us, length us, event | category | flops | bytes accessed | tf_op | source)
XLA Modules:
  0.0 88.4 jit_solution(6577577301272844515)
XLA Ops:
  0.1 1.3 %constant_dynamic-slice_fusion.1 = (bf16[256,1,128]{2,1,0:T(2,128)(2,1)S(1)}, bf16[256,1,128]{2,1,0:T(2,128)(2,1)S(1)}) fusion(bf16[256,2,128]{2,1,0:T(2,128)(2,1)} %param.7, s32[]{:T(128)S(6)} %select_n.24, bf16[256,2,128]{2,1,0:T(2,128)(2,1)} %param.6), kind=kLoop, calls=%fused_computation.15 | loop fusion | bytes 262148 | tf_op jit(solution)/shard_map/jit(dynamic_index_in_dim)/dynamic_slice | solution.py:310
  1.4 0.6 subtract_convert_fusion
  2.0 0.1 pad_maximum_fusion.3
  2.1 0.0 copy-start.1
  2.1 0.7 collective-permute-start.2
  2.8 5.8 %collective-permute-start.1 = (bf16[256,256]{1,0:T(8,128)(2,1)S(1)}, bf16[256,256]{1,0:T(8,128)(2,1)S(1)}, u32[]{:S(2)}, u32[]{:S(2)}) collective-permute-start(bf16[256,256]{1,0:T(8,128)(2,1)S(1)} %pad_maximum_fusion.3), channel_id=1, source_target_pairs={{0,32},{1,113},{2,34},{3,115},{4,36},{5,117},{6,38},{7,119},{8,40}... | collective-permute-start | bytes 393224 | tf_op jit(solution)/shard_map/ppermute | solution.py:44
  8.6 3.8 %collective-permute-start = (bf16[256,256]{1,0:T(8,128)(2,1)S(1)}, bf16[256,256]{1,0:T(8,128)(2,1)S(1)}, u32[]{:S(2)}, u32[]{:S(2)}) collective-permute-start(bf16[256,256]{1,0:T(8,128)(2,1)S(1)} %pad_maximum_fusion.3), channel_id=1, source_target_pairs={{0,16},{1,129},{2,18},{3,131},{4,20},{5,133},{6,22},{7,135},{8,24}... | collective-permute-start | bytes 393224 | tf_op jit(solution)/shard_map/ppermute | solution.py:44
  12.4 1.0 %turn.1 = bf16[128,1024]{1,0:T(8,128)(2,1)S(1)} custom-call(bf16[256,512]{1,0:T(8,128)(2,1)S(1)} %copy-done, f32[256,64]{1,0:T(8,128)S(1)} %get-tuple-element.40.cosine, f32[256,64]{1,0:T(8,128)S(1)} %get-tuple-element.39.sine), custom_call_target="tpu_custom_call" | custom-call | flops 1 | bytes 1 | tf_op jit(solution)/shard_map/turn/pallas_call | solution.py:196
  13.4 0.2 collective-permute-start.3
  13.7 0.0 collective-permute-done.2.rest_1_
  13.7 0.6 collective-permute-done.1
  14.3 3.3 %collective-permute-done = bf16[256,256]{1,0:T(8,128)(2,1)S(1)} collective-permute-done((bf16[256,256]{1,0:T(8,128)(2,1)S(1)}, bf16[256,256]{1,0:T(8,128)(2,1)S(1)}, u32[]{:S(2)}, u32[]{:S(2)}) %collective-permute-start) | collective-permute-done | bytes 131104 | tf_op jit(solution)/shard_map/ppermute | solution.py:44
  17.6 0.0 collective-permute-done.3
  17.6 0.1 collective-permute-start.11
  17.7 0.2 reduce-window.8
  17.9 0.1 select_reduce_fusion
  18.0 1.3 %collective-permute-start.10 = (bf16[640,256]{1,0:T(8,128)(2,1)S(1)}, bf16[640,256]{1,0:T(8,128)(2,1)S(1)}, u32[]{:S(2)}, u32[]{:S(2)}) collective-permute-start(bf16[640,256]{1,0:T(8,128)(2,1)S(1)} %pad_maximum_fusion.1), channel_id=1, source_target_pairs={{0,4},{1,5},{2,6},{3,7},{4,8},{5,9},{6,10},{7,11},{8,12},{9,13},{1... | collective-permute-start | bytes 983048 | tf_op jit(solution)/shard_map/ppermute | solution.py:44
  19.3 2.9 %collective-permute-start.9 = (bf16[640,256]{1,0:T(8,128)(2,1)S(1)}, bf16[640,256]{1,0:T(8,128)(2,1)S(1)}, u32[]{:S(2)}, u32[]{:S(2)}) collective-permute-start(bf16[640,256]{1,0:T(8,128)(2,1)S(1)} %pad_maximum_fusion.1), channel_id=1, source_target_pairs={{0,12},{1,13},{2,14},{3,15},{4,0},{5,1},{6,2},{7,3},{8,4},{9,5},{1... | collective-permute-start | bytes 983048 | tf_op jit(solution)/shard_map/ppermute | solution.py:44
  22.2 3.4 %collective-permute-start.4 = (bf16[512,256]{1,0:T(8,128)(2,1)S(1)}, bf16[512,256]{1,0:T(8,128)(2,1)S(1)}, u32[]{:S(2)}, u32[]{:S(2)}) collective-permute-start(bf16[512,256]{1,0:T(8,128)(2,1)S(1)} %pad_maximum_fusion.2.rest_1_), channel_id=1, source_target_pairs={{0,32},{1,225},{2,34},{3,227},{4,36},{5,229},{6,38},{7,231},{8,40}... | collective-permute-start | bytes 786440 | tf_op jit(solution)/shard_map/ppermute | solution.py:44
  25.6 1.4 %collective-permute-start.8 = (bf16[640,256]{1,0:T(8,128)(2,1)S(1)}, bf16[640,256]{1,0:T(8,128)(2,1)S(1)}, u32[]{:S(2)}, u32[]{:S(2)}) collective-permute-start(bf16[640,256]{1,0:T(8,128)(2,1)S(1)} %pad_maximum_fusion.1), channel_id=1, source_target_pairs={{0,8},{1,9},{2,10},{3,11},{4,12},{5,13},{6,14},{7,15},{8,0},{9,1},... | collective-permute-start | bytes 983048 | tf_op jit(solution)/shard_map/ppermute | solution.py:44
  27.1 2.2 %attend.6.rest_2_ = f32[136,2048]{1,0:T(8,128)S(1)} custom-call(bf16[128,2048]{1,0:T(8,128)(2,1)S(1)} %pad_maximum_fusion.q_ref, s32[8,2048]{1,0:T(8,128)S(1)} %broadcast_in_dim.25.low_ref, bf16[128,256]{1,0:T(8,128)(2,1)S(1)} %constant_dynamic-slice_fusion.rest_0_, bf16[512,256]{1,0:T(8,128)(2,1)S(1)} %pad_maximum_fusion.2.rest_1_), custom_call_target="tpu_custom_call" | custom-call | flops 1 | bytes 1 | tf_op jit(solution)/shard_map/attend/pallas_call | solution.py:175
  29.3 6.0 %collective-permute-done.4.rest_0_ = bf16[512,256]{1,0:T(8,128)(2,1)S(1)} collective-permute-done((bf16[512,256]{1,0:T(8,128)(2,1)S(1)}, bf16[512,256]{1,0:T(8,128)(2,1)S(1)}, u32[]{:S(2)}, u32[]{:S(2)}) %collective-permute-start.4) | collective-permute-done | bytes 262176 | tf_op jit(solution)/shard_map/ppermute | solution.py:44
  35.4 1.9 %collective-permute-start.7 = (bf16[512,256]{1,0:T(8,128)(2,1)S(1)}, bf16[512,256]{1,0:T(8,128)(2,1)S(1)}, u32[]{:S(2)}, u32[]{:S(2)}) collective-permute-start(bf16[512,256]{1,0:T(8,128)(2,1)S(1)} %collective-permute-done.4.rest_0_), channel_id=1, source_target_pairs={{0,12},{1,13},{2,14},{3,15},{4,0},{5,1},{6,2},{7,3},{8,4},{9,5},{1... | collective-permute-start | bytes 786440 | tf_op jit(solution)/shard_map/ppermute | solution.py:44
  37.3 0.1 collective-permute-start.6
  37.4 1.4 %collective-permute-start.5 = (bf16[512,256]{1,0:T(8,128)(2,1)S(1)}, bf16[512,256]{1,0:T(8,128)(2,1)S(1)}, u32[]{:S(2)}, u32[]{:S(2)}) collective-permute-start(bf16[512,256]{1,0:T(8,128)(2,1)S(1)} %collective-permute-done.4.rest_0_), channel_id=1, source_target_pairs={{0,8},{1,9},{2,10},{3,11},{4,12},{5,13},{6,14},{7,15},{8,0},{9,1},... | collective-permute-start | bytes 786440 | tf_op jit(solution)/shard_map/ppermute | solution.py:44
  38.8 4.3 %attend.7.rest_1_ = f32[136,2048]{1,0:T(8,128)S(1)} custom-call(bf16[128,2048]{1,0:T(8,128)(2,1)S(1)} %pad_maximum_fusion.q_ref, s32[8,2048]{1,0:T(8,128)S(1)} %broadcast_in_dim.25.low_ref, bf16[512,256]{1,0:T(8,128)(2,1)S(1)} %collective-permute-done.4.rest_0_, ...), custom_call_target="tpu_custom_call", output_to_operand_aliasing={{}: (4, {})} | custom-call | flops 1 | bytes 1 | tf_op jit(solution)/shard_map/attend/pallas_call | solution.py:175
  43.1 2.5 %attend.8.rest_2_ = f32[136,2048]{1,0:T(8,128)S(1)} custom-call(bf16[128,2048]{1,0:T(8,128)(2,1)S(1)} %pad_maximum_fusion.q_ref, s32[8,2048]{1,0:T(8,128)S(1)} %broadcast_in_dim.25.low_ref, bf16[640,256]{1,0:T(8,128)(2,1)S(1)} %collective-permute-done.9.rest_0_, f32[136,2048]{1,0:T(8,128)S(1)} %attend.7.rest_1_), custom_call_target="tpu_custom_call", output_to_operand_aliasing={{}: (3, {})} | custom-call | flops 1 | bytes 1 | tf_op jit(solution)/shard_map/attend/pallas_call | solution.py:175
  45.6 0.0 slice-start.1
  45.6 3.2 %attend.9.rest_2_ = f32[136,2048]{1,0:T(8,128)S(1)} custom-call(bf16[128,2048]{1,0:T(8,128)(2,1)S(1)} %pad_maximum_fusion.q_ref, s32[8,2048]{1,0:T(8,128)S(1)} %broadcast_in_dim.25.low_ref, bf16[640,256]{1,0:T(8,128)(2,1)S(1)} %collective-permute-done.8.rest_0_, bf16[256,256]{1,0:T(8,128)(2,1)S(1)} %collective-permute-done.2.rest_1_, ...), custom_call_target="tpu_custom_call", output_to_operand_aliasing={{}: (4, {})} | custom-call | flops 1 | bytes 1 | tf_op jit(solution)/shard_map/attend/pallas_call | solution.py:175
  48.8 1.6 %collective-permute-done.6.rest_0_ = bf16[512,256]{1,0:T(8,128)(2,1)S(1)} collective-permute-done((bf16[512,256]{1,0:T(8,128)(2,1)S(1)}, bf16[512,256]{1,0:T(8,128)(2,1)S(1)}, u32[]{:S(2)}, u32[]{:S(2)}) %collective-permute-start.6) | collective-permute-done | bytes 262176 | tf_op jit(solution)/shard_map/ppermute | solution.py:44
  50.4 3.8 %attend.10.rest_1_ = f32[136,2048]{1,0:T(8,128)S(1)} custom-call(bf16[128,2048]{1,0:T(8,128)(2,1)S(1)} %pad_maximum_fusion.q_ref, s32[8,2048]{1,0:T(8,128)S(1)} %broadcast_in_dim.25.low_ref, bf16[512,256]{1,0:T(8,128)(2,1)S(1)} %collective-permute-done.6.rest_0_, ...), custom_call_target="tpu_custom_call", output_to_operand_aliasing={{}: (4, {})} | custom-call | flops 1 | bytes 1 | tf_op jit(solution)/shard_map/attend/pallas_call | solution.py:175
  54.3 2.1 %attend.11.rest_0_ = f32[136,2048]{1,0:T(8,128)S(1)} custom-call(bf16[128,2048]{1,0:T(8,128)(2,1)S(1)} %pad_maximum_fusion.q_ref, s32[8,2048]{1,0:T(8,128)S(1)} %broadcast_in_dim.25.low_ref, bf16[512,256]{1,0:T(8,128)(2,1)S(1)} %collective-permute-done.5.rest_0_, f32[136,2048]{1,0:T(8,128)S(1)} %attend.10.rest_1_), custom_call_target="tpu_custom_call", output_to_operand_aliasing={{}: (3, {})} | custom-call | flops 1 | bytes 1 | tf_op jit(solution)/shard_map/attend/pallas_call | solution.py:175
  56.3 0.1 collective-permute-start.12
  56.4 2.7 %collective-permute-done.12.rest_1_ = f32[136,2048]{1,0:T(8,128)S(1)} collective-permute-done((f32[136,2048]{1,0:T(8,128)S(1)}, f32[136,2048]{1,0:T(8,128)S(1)}, u32[]{:S(2)}, u32[]{:S(2)}) %collective-permute-start.12) | collective-permute-done | bytes 1114144 | tf_op jit(solution)/shard_map/ppermute | solution.py:44
  59.2 1.7 %project.3 = (bf16[256,1024]{1,0:T(8,128)(2,1)S(1)}, bf16[256,512]{1,0:T(8,128)(2,1)S(1)}) custom-call(f32[136,2048]{1,0:T(8,128)S(1)} %attend.11.rest_0_, f32[136,2048]{1,0:T(8,128)S(1)} %collective-permute-done.12.rest_1_, bf16[512,8192]{1,0:T(8,128)(2,1)S(1)} %bitcast.14, bf16[512,8192]{1,0:T(8,128)(2,1)} %collective-permute-done.11.rest_3_.rest_2_), custom_call_target="tpu_custom_call" | custom-call | flops 1 | bytes 1 | tf_op jit(solution)/shard_map/project/pallas_call | solution.py:258
  60.9 1.5 %collective-permute-start.16 = (bf16[256,512]{1,0:T(8,128)(2,1)S(1)}, bf16[256,512]{1,0:T(8,128)(2,1)S(1)}, u32[]{:S(2)}, u32[]{:S(2)}) collective-permute-start(bf16[256,512]{1,0:T(8,128)(2,1)S(1)} %get-tuple-element.36), channel_id=1, source_target_pairs={{0,2},{1,3},{2,0},{3,1},{4,6},{5,7},{6,4},{7,5},{8,10},{9,11},{10,... | collective-permute-start | bytes 786440 | tf_op jit(solution)/shard_map/ppermute | solution.py:44
  62.4 2.5 %project.5 = (bf16[256,512]{1,0:T(8,128)(2,1)S(1)}, bf16[256,512]{1,0:T(8,128)(2,1)S(1)}, bf16[256,512]{1,0:T(8,128)(2,1)S(1)}) custom-call(bf16[256,1024]{1,0:T(8,128)(2,1)S(1)} %get-tuple-element.32.rest_0_, bf16[512,8192]{1,0:T(8,128)(2,1)S(1)} %bitcast.14, bf16[512,8192]{1,0:T(8,128)(2,1)} %collective-permute-done.11.rest_3_.rest_2_), custom_call_target="tpu_custom_call" | custom-call | flops 1 | bytes 1 | tf_op jit(solution)/shard_map/project/pallas_call | solution.py:258
  64.9 2.2 %collective-permute-start.15 = (bf16[256,512]{1,0:T(8,128)(2,1)S(1)}, bf16[256,512]{1,0:T(8,128)(2,1)S(1)}, u32[]{:S(2)}, u32[]{:S(2)}) collective-permute-start(bf16[256,512]{1,0:T(8,128)(2,1)S(1)} %get-tuple-element.35), channel_id=1, source_target_pairs={{0,2},{1,3},{2,0},{3,1},{4,6},{5,7},{6,4},{7,5},{8,10},{9,11},{10,... | collective-permute-start | bytes 786440 | tf_op jit(solution)/shard_map/ppermute | solution.py:44
  67.1 1.4 %collective-permute-start.14 = (bf16[256,512]{1,0:T(8,128)(2,1)S(1)}, bf16[256,512]{1,0:T(8,128)(2,1)S(1)}, u32[]{:S(2)}, u32[]{:S(2)}) collective-permute-start(bf16[256,512]{1,0:T(8,128)(2,1)S(1)} %get-tuple-element.34), channel_id=1, source_target_pairs={{0,2},{1,3},{2,0},{3,1},{4,6},{5,7},{6,4},{7,5},{8,10},{9,11},{10,... | collective-permute-start | bytes 786440 | tf_op jit(solution)/shard_map/ppermute | solution.py:44
  68.5 2.1 %collective-permute-start.13 = (bf16[256,512]{1,0:T(8,128)(2,1)S(1)}, bf16[256,512]{1,0:T(8,128)(2,1)S(1)}, u32[]{:S(2)}, u32[]{:S(2)}) collective-permute-start(bf16[256,512]{1,0:T(8,128)(2,1)S(1)} %get-tuple-element.33), channel_id=1, source_target_pairs={{0,2},{1,3},{2,0},{3,1},{4,6},{5,7},{6,4},{7,5},{8,10},{9,11},{10,... | collective-permute-start | bytes 786440 | tf_op jit(solution)/shard_map/ppermute | solution.py:44
  70.6 2.9 %project.4.kept = f32[256,2048]{1,0:T(8,128)S(1)} custom-call(bf16[256,1024]{1,0:T(8,128)(2,1)S(1)} %get-tuple-element.32.rest_0_, bf16[512,8192]{1,0:T(8,128)(2,1)S(1)} %bitcast.14, bf16[512,8192]{1,0:T(8,128)(2,1)} %collective-permute-done.11.rest_3_.rest_2_), custom_call_target="tpu_custom_call" | custom-call | flops 1 | bytes 1 | tf_op jit(solution)/shard_map/project/pallas_call | solution.py:258
  73.6 0.7 finish.4.rest_0_
  74.3 2.9 %collective-permute-done.15.received = bf16[256,512]{1,0:T(8,128)(2,1)S(1)} collective-permute-done((bf16[256,512]{1,0:T(8,128)(2,1)S(1)}, bf16[256,512]{1,0:T(8,128)(2,1)S(1)}, u32[]{:S(2)}, u32[]{:S(2)}) %collective-permute-start.15) | collective-permute-done | bytes 262176 | tf_op jit(solution)/shard_map/ppermute | solution.py:44
  77.2 0.7 finish.5.rest_0_
  78.0 4.9 %collective-permute-done.14.received = bf16[256,512]{1,0:T(8,128)(2,1)S(1)} collective-permute-done((bf16[256,512]{1,0:T(8,128)(2,1)S(1)}, bf16[256,512]{1,0:T(8,128)(2,1)S(1)}, u32[]{:S(2)}, u32[]{:S(2)}) %collective-permute-start.14) | collective-permute-done | bytes 262176 | tf_op jit(solution)/shard_map/ppermute | solution.py:44
  82.9 0.7 finish.6.rest_0_
  83.6 4.1 %collective-permute-done.13.received = bf16[256,512]{1,0:T(8,128)(2,1)S(1)} collective-permute-done((bf16[256,512]{1,0:T(8,128)(2,1)S(1)}, bf16[256,512]{1,0:T(8,128)(2,1)S(1)}, u32[]{:S(2)}, u32[]{:S(2)}) %collective-permute-start.13) | collective-permute-done | bytes 262176 | tf_op jit(solution)/shard_map/ppermute | solution.py:44
  87.7 0.7 finish.7
  (25 shorter events, 0.2 us)
Async XLA Ops:
  0.0 12.4 %copy-start = (bf16[256,512]{1,0:T(8,128)(2,1)S(1)}, bf16[256,512]{1,0:T(8,128)(2,1)}, u32[]{:S(2)}) copy-start(bf16[256,512]{1,0:T(8,128)(2,1)} %queries.1) | copy-start | bytes 786436
  2.1 15.6 %copy-start.1 = (s32[8]{0:T(128)S(1)}, s32[8]{0:T(128)}, u32[]{:S(2)}) copy-start(s32[8]{0:T(128)} %param.8) | copy-start | bytes 100
  2.1 11.6 %collective-permute-start.2 = (bf16[256,256]{1,0:T(8,128)(2,1)S(1)}, bf16[256,256]{1,0:T(8,128)(2,1)S(1)}, u32[]{:S(2)}, u32[]{:S(2)}) collective-permute-start(bf16[256,256]{1,0:T(8,128)(2,1)S(1)} %pad_maximum_fusion.3), channel_id=1, source_target_pairs={{12,144},{14,146},{28,160},{30,162},{44,176},{46,178},{60,192},{62... | collective-permute-start | bytes 393224 | tf_op jit(solution)/shard_map/ppermute | solution.py:44
  2.8 11.5 %collective-permute-start.1 = (bf16[256,256]{1,0:T(8,128)(2,1)S(1)}, bf16[256,256]{1,0:T(8,128)(2,1)S(1)}, u32[]{:S(2)}, u32[]{:S(2)}) collective-permute-start(bf16[256,256]{1,0:T(8,128)(2,1)S(1)} %pad_maximum_fusion.3), channel_id=1, source_target_pairs={{0,32},{1,113},{2,34},{3,115},{4,36},{5,117},{6,38},{7,119},{8,40}... | collective-permute-start | bytes 393224 | tf_op jit(solution)/shard_map/ppermute | solution.py:44
  8.6 9.0 %collective-permute-start = (bf16[256,256]{1,0:T(8,128)(2,1)S(1)}, bf16[256,256]{1,0:T(8,128)(2,1)S(1)}, u32[]{:S(2)}, u32[]{:S(2)}) collective-permute-start(bf16[256,256]{1,0:T(8,128)(2,1)S(1)} %pad_maximum_fusion.3), channel_id=1, source_target_pairs={{0,16},{1,129},{2,18},{3,131},{4,20},{5,133},{6,22},{7,135},{8,24}... | collective-permute-start | bytes 393224 | tf_op jit(solution)/shard_map/ppermute | solution.py:44
  13.4 4.2 %collective-permute-start.3 = (bf16[128,1024]{1,0:T(8,128)(2,1)S(1)}, bf16[128,1024]{1,0:T(8,128)(2,1)S(1)}, u32[]{:S(2)}, u32[]{:S(2)}) collective-permute-start(bf16[128,1024]{1,0:T(8,128)(2,1)S(1)} %turn.1), channel_id=1, source_target_pairs={{0,1},{1,0},{2,3},{3,2},{4,5},{5,4},{6,7},{7,6},{8,9},{9,8},{10,11... | collective-permute-start | bytes 786440 | tf_op jit(solution)/shard_map/ppermute | solution.py:44
  17.6 31.2 %collective-permute-start.11 = (bf16[512,8192]{1,0:T(8,128)(2,1)}, bf16[512,8192]{1,0:T(8,128)(2,1)}, u32[]{:S(2)}, u32[]{:S(2)}) collective-permute-start(bf16[512,8192]{1,0:T(8,128)(2,1)} %rest_1_.1), channel_id=1, source_target_pairs={{0,1},{1,0},{2,3},{3,2},{4,5},{5,4},{6,7},{7,6},{8,9},{9,8},{10,11... | collective-permute-start | bytes 25165832 | tf_op jit(solution)/shard_map/ppermute | solution.py:44
  18.0 19.3 %collective-permute-start.10 = (bf16[640,256]{1,0:T(8,128)(2,1)S(1)}, bf16[640,256]{1,0:T(8,128)(2,1)S(1)}, u32[]{:S(2)}, u32[]{:S(2)}) collective-permute-start(bf16[640,256]{1,0:T(8,128)(2,1)S(1)} %pad_maximum_fusion.1), channel_id=1, source_target_pairs={{0,4},{1,5},{2,6},{3,7},{4,8},{5,9},{6,10},{7,11},{8,12},{9,13},{1... | collective-permute-start | bytes 983048 | tf_op jit(solution)/shard_map/ppermute | solution.py:44
  19.3 18.1 %collective-permute-start.9 = (bf16[640,256]{1,0:T(8,128)(2,1)S(1)}, bf16[640,256]{1,0:T(8,128)(2,1)S(1)}, u32[]{:S(2)}, u32[]{:S(2)}) collective-permute-start(bf16[640,256]{1,0:T(8,128)(2,1)S(1)} %pad_maximum_fusion.1), channel_id=1, source_target_pairs={{0,12},{1,13},{2,14},{3,15},{4,0},{5,1},{6,2},{7,3},{8,4},{9,5},{1... | collective-permute-start | bytes 983048 | tf_op jit(solution)/shard_map/ppermute | solution.py:44
  22.2 13.2 %collective-permute-start.4 = (bf16[512,256]{1,0:T(8,128)(2,1)S(1)}, bf16[512,256]{1,0:T(8,128)(2,1)S(1)}, u32[]{:S(2)}, u32[]{:S(2)}) collective-permute-start(bf16[512,256]{1,0:T(8,128)(2,1)S(1)} %pad_maximum_fusion.2.rest_1_), channel_id=1, source_target_pairs={{0,32},{1,225},{2,34},{3,227},{4,36},{5,229},{6,38},{7,231},{8,40}... | collective-permute-start | bytes 786440 | tf_op jit(solution)/shard_map/ppermute | solution.py:44
  25.6 20.0 %collective-permute-start.8 = (bf16[640,256]{1,0:T(8,128)(2,1)S(1)}, bf16[640,256]{1,0:T(8,128)(2,1)S(1)}, u32[]{:S(2)}, u32[]{:S(2)}) collective-permute-start(bf16[640,256]{1,0:T(8,128)(2,1)S(1)} %pad_maximum_fusion.1), channel_id=1, source_target_pairs={{0,8},{1,9},{2,10},{3,11},{4,12},{5,13},{6,14},{7,15},{8,0},{9,1},... | collective-permute-start | bytes 983048 | tf_op jit(solution)/shard_map/ppermute | solution.py:44
  35.4 13.5 %collective-permute-start.7 = (bf16[512,256]{1,0:T(8,128)(2,1)S(1)}, bf16[512,256]{1,0:T(8,128)(2,1)S(1)}, u32[]{:S(2)}, u32[]{:S(2)}) collective-permute-start(bf16[512,256]{1,0:T(8,128)(2,1)S(1)} %collective-permute-done.4.rest_0_), channel_id=1, source_target_pairs={{0,12},{1,13},{2,14},{3,15},{4,0},{5,1},{6,2},{7,3},{8,4},{9,5},{1... | collective-permute-start | bytes 786440 | tf_op jit(solution)/shard_map/ppermute | solution.py:44
  37.3 13.1 %collective-permute-start.6 = (bf16[512,256]{1,0:T(8,128)(2,1)S(1)}, bf16[512,256]{1,0:T(8,128)(2,1)S(1)}, u32[]{:S(2)}, u32[]{:S(2)}) collective-permute-start(bf16[512,256]{1,0:T(8,128)(2,1)S(1)} %collective-permute-done.4.rest_0_), channel_id=1, source_target_pairs={{0,4},{1,5},{2,6},{3,7},{4,8},{5,9},{6,10},{7,11},{8,12},{9,13},{1... | collective-permute-start | bytes 786440 | tf_op jit(solution)/shard_map/ppermute | solution.py:44
  37.4 16.9 %collective-permute-start.5 = (bf16[512,256]{1,0:T(8,128)(2,1)S(1)}, bf16[512,256]{1,0:T(8,128)(2,1)S(1)}, u32[]{:S(2)}, u32[]{:S(2)}) collective-permute-start(bf16[512,256]{1,0:T(8,128)(2,1)S(1)} %collective-permute-done.4.rest_0_), channel_id=1, source_target_pairs={{0,8},{1,9},{2,10},{3,11},{4,12},{5,13},{6,14},{7,15},{8,0},{9,1},... | collective-permute-start | bytes 786440 | tf_op jit(solution)/shard_map/ppermute | solution.py:44
  38.8 20.4 %slice-start = ((s8[8388608]{0:T(1024)(128)(4,1)}), s8[4194304]{0:T(1024)(128)(4,1)S(1)}, s32[]{:S(2)}) async-start(s8[8388608]{0:T(1024)(128)(4,1)} %bitcast.13), calls=%async_computation | async-start | bytes 8388608
  45.6 13.6 %slice-start.1 = ((s8[8388608]{0:T(1024)(128)(4,1)}), s8[4194304]{0:T(1024)(128)(4,1)S(1)}, s32[]{:S(2)}) async-start(s8[8388608]{0:T(1024)(128)(4,1)} %bitcast.13), calls=%async_computation.1 | async-start | bytes 8388608
  56.3 2.8 %collective-permute-start.12 = (f32[136,2048]{1,0:T(8,128)S(1)}, f32[136,2048]{1,0:T(8,128)S(1)}, u32[]{:S(2)}, u32[]{:S(2)}) collective-permute-start(f32[136,2048]{1,0:T(8,128)S(1)} %attend.11.rest_0_), channel_id=1, source_target_pairs={{0,1},{1,0},{2,3},{3,2},{4,5},{5,4},{6,7},{7,6},{8,9},{9,8},{10,11... | collective-permute-start | bytes 3342344 | tf_op jit(solution)/shard_map/ppermute | solution.py:44
  60.9 12.7 %collective-permute-start.16 = (bf16[256,512]{1,0:T(8,128)(2,1)S(1)}, bf16[256,512]{1,0:T(8,128)(2,1)S(1)}, u32[]{:S(2)}, u32[]{:S(2)}) collective-permute-start(bf16[256,512]{1,0:T(8,128)(2,1)S(1)} %get-tuple-element.36), channel_id=1, source_target_pairs={{0,2},{1,3},{2,0},{3,1},{4,6},{5,7},{6,4},{7,5},{8,10},{9,11},{10,... | collective-permute-start | bytes 786440 | tf_op jit(solution)/shard_map/ppermute | solution.py:44
  64.9 12.4 %collective-permute-start.15 = (bf16[256,512]{1,0:T(8,128)(2,1)S(1)}, bf16[256,512]{1,0:T(8,128)(2,1)S(1)}, u32[]{:S(2)}, u32[]{:S(2)}) collective-permute-start(bf16[256,512]{1,0:T(8,128)(2,1)S(1)} %get-tuple-element.35), channel_id=1, source_target_pairs={{0,2},{1,3},{2,0},{3,1},{4,6},{5,7},{6,4},{7,5},{8,10},{9,11},{10,... | collective-permute-start | bytes 786440 | tf_op jit(solution)/shard_map/ppermute | solution.py:44
  67.1 15.8 %collective-permute-start.14 = (bf16[256,512]{1,0:T(8,128)(2,1)S(1)}, bf16[256,512]{1,0:T(8,128)(2,1)S(1)}, u32[]{:S(2)}, u32[]{:S(2)}) collective-permute-start(bf16[256,512]{1,0:T(8,128)(2,1)S(1)} %get-tuple-element.34), channel_id=1, source_target_pairs={{0,2},{1,3},{2,0},{3,1},{4,6},{5,7},{6,4},{7,5},{8,10},{9,11},{10,... | collective-permute-start | bytes 786440 | tf_op jit(solution)/shard_map/ppermute | solution.py:44
  68.5 19.2 %collective-permute-start.13 = (bf16[256,512]{1,0:T(8,128)(2,1)S(1)}, bf16[256,512]{1,0:T(8,128)(2,1)S(1)}, u32[]{:S(2)}, u32[]{:S(2)}) collective-permute-start(bf16[256,512]{1,0:T(8,128)(2,1)S(1)} %get-tuple-element.33), channel_id=1, source_target_pairs={{0,2},{1,3},{2,0},{3,1},{4,6},{5,7},{6,4},{7,5},{8,10},{9,11},{10,... | collective-permute-start | bytes 786440 | tf_op jit(solution)/shard_map/ppermute | solution.py:44

commit v2 on v1

--- a/solution.py
+++ b/solution.py
@@ -26,6 +26,7 @@
 TILE = 512
 NOWHERE = -(1 << 24)
 OUT_COLUMNS = 2048
+HALF = BLOCK // 2
 MIB = 1024 * 1024
 
 
@@ -110,7 +111,7 @@
     return (jnp.where(core == 0, row - kind, row - 9 + kind) * ROW + at) * BLOCK, BLOCK
 
 
-def attend_kernel(kinds, fresh, q_ref, low_ref, *rest):
+def attend_kernel(kinds, fresh, first_lane, q_ref, low_ref, *rest):
     state = rest[-1]
     kept, refs = (None, rest[:-1]) if fresh else (rest[-2], rest[:-2])
     scale = HD**-0.5 * LOG2E
@@ -127,16 +128,20 @@
         bases.append(base)
         none = (low_first >= base + size) & none
 
+    width = state.shape[1]
+    lanes = slice(first_lane, first_lane + width)
+
     def step():
-        q = q_ref[...]
-        low = low_ref[0:1, :]
+        q = q_ref[:, lanes]
+        low = low_ref[0:1, lanes]
         scores = []
         for part, base, kind in zip(parts, bases, kinds):
             s = jnp.dot(part[:, :HD], q, preferred_element_type=jnp.float32)
             at = lax.broadcasted_iota(jnp.int32, s.shape, 0)
             live = at >= low - base
             if kind == ("half", 0):
-                query = lax.broadcasted_iota(jnp.int32, (1, LANES), 1) % BLOCK + first_query
+                lane = lax.broadcasted_iota(jnp.int32, (1, width), 1) + first_lane
+                query = lane // (LANES // 2) * HALF + lane % HALF + first_query
                 live = live & (at <= query - base)
             scores.append(jnp.where(live, s, MASKED))
         s = jnp.concatenate(scores, axis=0) if len(scores) > 1 else scores[0]
@@ -144,7 +149,7 @@
         values = jnp.concatenate(values, axis=1) if len(values) > 1 else values[0]
         values = jnp.concatenate([values, jnp.ones((16, values.shape[1]), jnp.bfloat16)], axis=0)
         peak = jnp.max(s, axis=0, keepdims=True) * scale
-        old = jnp.full_like(peak, EMPTY) if fresh else kept[HD : HD + 1, :]
+        old = jnp.full_like(peak, EMPTY) if fresh else kept[HD : HD + 1, lanes]
         new = jnp.maximum(old, peak)
         weights = jnp.exp2(s * scale - new).astype(jnp.bfloat16)
         summed = jnp.dot(values, weights, preferred_element_type=jnp.float32)
@@ -152,10 +157,10 @@
         summed = summed[:HD]
         if not fresh:
             alpha = jnp.exp2(old - new)
-            summed = summed + kept[:HD, :] * alpha
-            denom = denom + kept[HD + 1 : HD + 2, :] * alpha
+            summed = summed + kept[:HD, lanes] * alpha
+            denom = denom + kept[HD + 1 : HD + 2, lanes] * alpha
         state[:HD, :] = summed
-        state[HD:, :] = jnp.concatenate([new, denom, jnp.zeros((6, LANES), jnp.float32)], axis=0)
+        state[HD:, :] = jnp.concatenate([new, denom, jnp.zeros((6, width), jnp.float32)], axis=0)
 
     if fresh:
         step()
@@ -163,33 +168,37 @@
 
         @pl.when(none)
         def _():
-            state[...] = kept[...]
+            state[...] = kept[:, lanes]
 
         @pl.when(jnp.logical_not(none))
         def _():
             step()
 
 
-def attend(q_all, low, refs, kinds, state=None):
+def attend(q_all, low, refs, kinds, state=None, half=None):
     operands = list(refs) + ([] if state is None else [state])
+    width, first_lane = (LANES, 0) if half is None else (LANES // 2, half * LANES // 2)
+    in_place = state is not None and half is None
     return pl.pallas_call(
-        functools.partial(attend_kernel, kinds, state is None),
-        out_shape=jax.ShapeDtypeStruct((STATE, LANES), jnp.float32),
+        functools.partial(attend_kernel, kinds, state is None, first_lane),
+        out_shape=jax.ShapeDtypeStruct((STATE, width), jnp.float32),
         in_specs=[pl.BlockSpec(memory_space=pltpu.VMEM)] * (2 + len(operands)),
         out_specs=pl.BlockSpec(memory_space=pltpu.VMEM),
-        input_output_aliases={} if state is None else {1 + len(operands): 0},
-        compiler_params=pltpu.CompilerParams(vmem_limit_bytes=32 * MIB),
+        input_output_aliases={1 + len(operands): 0} if in_place else {},
+        compiler_params=pltpu.CompilerParams(vmem_limit_bytes=24 * MIB),
         cost_estimate=pl.CostEstimate(flops=1, bytes_accessed=1, transcendentals=0),
         name="attend",
     )(q_all, low, *operands)
 
 
 def turn_kernel(queries, cosine, sine, out):
-    half = HD // 2
-    for h in range(queries.shape[1] // HD):
+    heads = queries.shape[1] // HD
+    for h in range(heads):
         x = queries[:, h * HD : (h + 1) * HD].astype(jnp.float32)
-        turned = rope(x, cosine[...], sine[...]).astype(jnp.bfloat16)
-        out[:, h * BLOCK : (h + 1) * BLOCK] = turned.T
+        turned = rope(x, cosine[...], sine[...]).astype(jnp.bfloat16).T
+        for half in range(2):
+            at = (half * heads + h) * HALF
+            out[:, at : at + HALF] = turned[:, half * HALF : (half + 1) * HALF]
 
 
 def turn(queries, cosine, sine):
@@ -206,9 +215,9 @@
 
 def merged(mine, theirs, out):
     for h in range(HEADS):
-        a = slice(h * BLOCK, (h + 1) * BLOCK)
+        a = slice(h * HALF, (h + 1) * HALF)
         g = (h + HEADS // 2) % HEADS
-        b = slice(g * BLOCK, (g + 1) * BLOCK)
+        b = slice(g * HALF, (g + 1) * HALF)
         peak_a, peak_b = mine[HD : HD + 1, a], theirs[HD : HD + 1, b]
         peak = jnp.maximum(peak_a, peak_b)
         scale_a, scale_b = jnp.exp2(peak_a - peak), jnp.exp2(peak_b - peak)
@@ -250,9 +259,9 @@
 
 def project(operands, weights, other_side, first, widths, dtype, merging=False):
     half = HEADS * HD // 2
-    shapes = [jax.ShapeDtypeStruct((BLOCK, width), dtype) for width in widths]
+    shapes = [jax.ShapeDtypeStruct((HALF, width), dtype) for width in widths]
     if merging:
-        shapes = [jax.ShapeDtypeStruct((BLOCK, 2 * half), jnp.bfloat16)] + shapes
+        shapes = [jax.ShapeDtypeStruct((HALF, 2 * half), jnp.bfloat16)] + shapes
     pieces = sum(widths) // TILE
     vmem = pl.BlockSpec(memory_space=pltpu.VMEM)
     return pl.pallas_call(
@@ -265,7 +274,7 @@
             pltpu.VMEM((pieces, 2, half, TILE), jnp.bfloat16),
             pltpu.SemaphoreType.DMA((pieces, 2)),
         ],
-        compiler_params=pltpu.CompilerParams(vmem_limit_bytes=32 * MIB),
+        compiler_params=pltpu.CompilerParams(vmem_limit_bytes=16 * MIB),
         cost_estimate=pl.CostEstimate(flops=1, bytes_accessed=1, transcendentals=0),
         name="project",
     )(*operands, *weights)
@@ -275,25 +284,25 @@
     rest[-1][...] = (kept[...] + received[...].astype(jnp.float32)).astype(jnp.bfloat16)
 
 
-def finish(kept, received, first, out):
+def finish(kept, received, half, first, out):
     columns, start = received.shape[1], first // TILE
-    tile = pl.BlockSpec((BLOCK, TILE), lambda j: (0, start + j))
-    in_specs = [tile, pl.BlockSpec((BLOCK, TILE), lambda j: (0, j))]
+    in_specs = [
+        pl.BlockSpec((HALF, TILE), lambda j: (0, start + j)),
+        pl.BlockSpec((HALF, TILE), lambda j: (0, j)),
+    ]
     operands = [kept, received]
     if out is not None:
         in_specs.append(pl.BlockSpec(memory_space=pl.ANY))
         operands.append(out)
     return pl.pallas_call(
         finish_kernel,
-        out_shape=jax.ShapeDtypeStruct(kept.shape, jnp.bfloat16),
+        out_shape=jax.ShapeDtypeStruct((BLOCK, OUT_COLUMNS), jnp.bfloat16),
         grid=(columns // TILE,),
         in_specs=in_specs,
-        out_specs=tile,
+        out_specs=pl.BlockSpec((HALF, TILE), lambda j: (half, start + j)),
         input_output_aliases={} if out is None else {2: 0},
-        compiler_params=pltpu.CompilerParams(vmem_limit_bytes=32 * MIB),
-        cost_estimate=pl.CostEstimate(
-            flops=BLOCK * columns, bytes_accessed=8 * BLOCK * columns, transcendentals=0
-        ),
+        compiler_params=pltpu.CompilerParams(vmem_limit_bytes=16 * MIB),
+        cost_estimate=pl.CostEstimate(flops=1, bytes_accessed=1, transcendentals=0),
         name="finish",
     )(*operands)
 
@@ -326,10 +335,14 @@
     group_2 = permute(near, two_rows_on)
     columns_1 = [permute(group_1, in_row(shift)) for shift in shifts]
 
-    q_all = jnp.concatenate([q_own, q_other], axis=1)
+    own_lanes = LANES // 4
+    q_all = jnp.concatenate(
+        [q[:, i * own_lanes : (i + 1) * own_lanes] for i in range(2) for q in (q_own, q_other)],
+        axis=1,
+    )
     doc_ends = jnp.cumsum(doc_lengths)
     low = jnp.max(jnp.where(doc_ends[:, None] <= query_pos[None], doc_ends[:, None], 0), axis=0)
-    low = jnp.broadcast_to(low, (8, HEADS, BLOCK)).reshape(8, LANES)
+    low = jnp.broadcast_to(low.reshape(2, 1, HALF), (8, 2, HEADS, HALF)).reshape(8, LANES)
     step = functools.partial(attend, q_all, low)
 
     state = step([half, near], [("half", 0), (1, 0), (2, 0)])
@@ -345,19 +358,26 @@
         state = step(refs, kinds, state)
     state, other_weight = lax.optimization_barrier((state, other_weight))
     weights = (out_weight, other_weight)
-    state = step(columns_2[:2], rows_2(1) + rows_2(-1), state)
-    state = step(columns_2[2:], rows_2(2), state)
-
-    theirs = permute(state, other_core)
-    attended, partial = project((state, theirs), weights, True, 0, (512,), jnp.bfloat16, True)
-    received = [permute(partial, other_hi)]
-    for partial in project((attended,), weights, True, 512, (512,) * 3, jnp.bfloat16):
-        received.append(permute(partial, other_hi))
-    (kept,) = project((attended,), weights, False, 0, (OUT_COLUMNS,), jnp.float32)
-    out, first = None, 0
-    for piece in received:
-        out = finish(kept, piece, first, out)
-        first += piece.shape[1]
+    state = step(columns_2[:1], rows_2(1), state)
+    halves = []
+    for half in range(2):
+        mine = step(columns_2[1:], rows_2(-1) + rows_2(2), state, half)
+        halves.append((mine, permute(mine, other_core)))
+
+    sent, kept = [], []
+    for half, (first, rest) in enumerate((((OUT_COLUMNS,), ()), ((1024,), (1024,)))):
+        attended, partial = project(halves[half], weights, True, 0, first, jnp.bfloat16, True)
+        partials = [partial]
+        if rest:
+            partials += project((attended,), weights, True, first[0], rest, jnp.bfloat16)
+        sent.append([permute(partial, other_hi) for partial in partials])
+        kept += project((attended,), weights, False, 0, (OUT_COLUMNS,), jnp.float32)
+    out = None
+    for half in range(2):
+        first = 0
+        for piece in sent[half]:
+            out = finish(kept[half], piece, half, first, out)
+            first += piece.shape[1]
     return out
 
 

time: 88.7 us -> 89.8 us (1.012)
  Pallas kernels: 29.3 us -> 33.6 us
  waiting for transfers between devices: 26.1 us -> 22 us
    ppermute x17, waiting for transfers between devices: 26.1 us -> 22 us  [permute(): return lax.ppermute(x, ('seq', 'tensor'), device_perm(move))]
    pallas_call x3 -> x5, Pallas kernels: 7.1 us -> 11 us  [project(): pl.pallas_call(functools.partial(project_kernel, other_side, first, mergi...]
  transfers between devices with their start and end apart: 17 -> 17, of which waited for: 8 -> 6; matrix products, arithmetic and copies ran while one was open for 0% -> 0% of each run, Pallas kernels for 28% -> 35%
where the time goes in v2:
time: 89.8 us; the launch traced here: 88.7 us
  Pallas kernels  33.6 us (37%)
  starting transfers between devices  30.2 us (34%)
  waiting for transfers between devices  22 us (24%)
  local copies, waits for them, and re-layouts  1.37 us (2%)
  other arithmetic  1.07 us (1%)
    ppermute x17, starting transfers between devices, permute(): return lax.ppermute(x, ('seq', 'tensor'), device_perm(move))  30.2 us
    ppermute x17, waiting for transfers between devices, permute(): return lax.ppermute(x, ('seq', 'tensor'), device_perm(move))  22 us
    pallas_call x7, Pallas kernels, attend(): pl.pallas_call(functools.partial(attend_kernel, kinds, state is None, fir...  18.5 us
    pallas_call x5, Pallas kernels, project(): pl.pallas_call(functools.partial(project_kernel, other_side, first, mergi...  11 us
    pallas_call x3, Pallas kernels, finish(): pl.pallas_call(finish_kernel, out_shape=jax.ShapeDtypeStruct((BLOCK, OUT_...  3.11 us
  transfers between devices with their start and end apart: 17, of which 6 were waited for; matrix products, arithmetic and copies ran while one was open for 0% of the time, Pallas kernels for 35%

profile of v2, /device:TPU:6, one launch (start us, length us, event | category | flops | bytes accessed | tf_op | source)
XLA Modules:
  0.0 88.7 jit_solution(4604508761327100413)
XLA Ops:
  0.1 1.3 %constant_dynamic-slice_fusion.1 = (bf16[256,1,128]{2,1,0:T(2,128)(2,1)S(1)}, bf16[256,1,128]{2,1,0:T(2,128)(2,1)S(1)}) fusion(bf16[256,2,128]{2,1,0:T(2,128)(2,1)} %param.7, s32[]{:T(128)S(6)} %select_n.24, bf16[256,2,128]{2,1,0:T(2,128)(2,1)} %param.6), kind=kLoop, calls=%fused_computation.15 | loop fusion | bytes 262148 | tf_op jit(solution)/shard_map/jit(dynamic_index_in_dim)/dynamic_slice | solution.py:319
  1.4 0.6 subtract_convert_fusion
  2.0 0.1 pad_maximum_fusion.3
  2.1 0.0 copy-start.1
  2.1 0.7 collective-permute-start.2
  2.8 5.8 %collective-permute-start.1 = (bf16[256,256]{1,0:T(8,128)(2,1)S(1)}, bf16[256,256]{1,0:T(8,128)(2,1)S(1)}, u32[]{:S(2)}, u32[]{:S(2)}) collective-permute-start(bf16[256,256]{1,0:T(8,128)(2,1)S(1)} %pad_maximum_fusion.3), channel_id=1, source_target_pairs={{0,32},{1,113},{2,34},{3,115},{4,36},{5,117},{6,38},{7,119},{8,40}... | collective-permute-start | bytes 393224 | tf_op jit(solution)/shard_map/ppermute | solution.py:45
  8.6 3.8 %collective-permute-start = (bf16[256,256]{1,0:T(8,128)(2,1)S(1)}, bf16[256,256]{1,0:T(8,128)(2,1)S(1)}, u32[]{:S(2)}, u32[]{:S(2)}) collective-permute-start(bf16[256,256]{1,0:T(8,128)(2,1)S(1)} %pad_maximum_fusion.3), channel_id=1, source_target_pairs={{0,16},{1,129},{2,18},{3,131},{4,20},{5,133},{6,22},{7,135},{8,24}... | collective-permute-start | bytes 393224 | tf_op jit(solution)/shard_map/ppermute | solution.py:45
  12.4 1.0 %turn.1 = bf16[128,1024]{1,0:T(8,128)(2,1)S(1)} custom-call(bf16[256,512]{1,0:T(8,128)(2,1)S(1)} %copy-done, f32[256,64]{1,0:T(8,128)S(1)} %get-tuple-element.42.cosine, f32[256,64]{1,0:T(8,128)S(1)} %get-tuple-element.41.sine), custom_call_target="tpu_custom_call" | custom-call | flops 1 | bytes 1 | tf_op jit(solution)/shard_map/turn/pallas_call | solution.py:205
  13.4 0.2 collective-permute-start.3
  13.7 0.0 collective-permute-done.2.rest_1_
  13.7 0.6 collective-permute-done.1
  14.3 3.3 %collective-permute-done = bf16[256,256]{1,0:T(8,128)(2,1)S(1)} collective-permute-done((bf16[256,256]{1,0:T(8,128)(2,1)S(1)}, bf16[256,256]{1,0:T(8,128)(2,1)S(1)}, u32[]{:S(2)}, u32[]{:S(2)}) %collective-permute-start) | collective-permute-done | bytes 131104 | tf_op jit(solution)/shard_map/ppermute | solution.py:45
  17.6 0.0 collective-permute-done.3
  17.6 0.1 collective-permute-start.11
  17.7 0.2 reduce-window.8
  17.9 0.1 select_reduce_fusion
  18.0 1.3 %collective-permute-start.10 = (bf16[640,256]{1,0:T(8,128)(2,1)S(1)}, bf16[640,256]{1,0:T(8,128)(2,1)S(1)}, u32[]{:S(2)}, u32[]{:S(2)}) collective-permute-start(bf16[640,256]{1,0:T(8,128)(2,1)S(1)} %pad_maximum_fusion.1), channel_id=1, source_target_pairs={{0,4},{1,5},{2,6},{3,7},{4,8},{5,9},{6,10},{7,11},{8,12},{9,13},{1... | collective-permute-start | bytes 983048 | tf_op jit(solution)/shard_map/ppermute | solution.py:45
  19.3 2.9 %collective-permute-start.9 = (bf16[640,256]{1,0:T(8,128)(2,1)S(1)}, bf16[640,256]{1,0:T(8,128)(2,1)S(1)}, u32[]{:S(2)}, u32[]{:S(2)}) collective-permute-start(bf16[640,256]{1,0:T(8,128)(2,1)S(1)} %pad_maximum_fusion.1), channel_id=1, source_target_pairs={{0,12},{1,13},{2,14},{3,15},{4,0},{5,1},{6,2},{7,3},{8,4},{9,5},{1... | collective-permute-start | bytes 983048 | tf_op jit(solution)/shard_map/ppermute | solution.py:45
  22.2 1.4 %collective-permute-start.8 = (bf16[640,256]{1,0:T(8,128)(2,1)S(1)}, bf16[640,256]{1,0:T(8,128)(2,1)S(1)}, u32[]{:S(2)}, u32[]{:S(2)}) collective-permute-start(bf16[640,256]{1,0:T(8,128)(2,1)S(1)} %pad_maximum_fusion.1), channel_id=1, source_target_pairs={{0,8},{1,9},{2,10},{3,11},{4,12},{5,13},{6,14},{7,15},{8,0},{9,1},... | collective-permute-start | bytes 983048 | tf_op jit(solution)/shard_map/ppermute | solution.py:45
  23.6 3.3 %collective-permute-start.4 = (bf16[512,256]{1,0:T(8,128)(2,1)S(1)}, bf16[512,256]{1,0:T(8,128)(2,1)S(1)}, u32[]{:S(2)}, u32[]{:S(2)}) collective-permute-start(bf16[512,256]{1,0:T(8,128)(2,1)S(1)} %pad_maximum_fusion.2.rest_1_), channel_id=1, source_target_pairs={{0,32},{1,225},{2,34},{3,227},{4,36},{5,229},{6,38},{7,231},{8,40}... | collective-permute-start | bytes 786440 | tf_op jit(solution)/shard_map/ppermute | solution.py:45
  27.1 2.2 %attend.7.rest_2_ = f32[136,2048]{1,0:T(8,128)S(1)} custom-call(bf16[128,2048]{1,0:T(8,128)(2,1)S(1)} %pad_maximum_fusion.q_ref, s32[8,2048]{1,0:T(8,128)S(1)} %broadcast_in_dim.27.low_ref, bf16[128,256]{1,0:T(8,128)(2,1)S(1)} %constant_dynamic-slice_fusion.rest_0_, bf16[512,256]{1,0:T(8,128)(2,1)S(1)} %pad_maximum_fusion.2.rest_1_), custom_call_target="tpu_custom_call" | custom-call | flops 1 | bytes 1 | tf_op jit(solution)/shard_map/attend/pallas_call | solution.py:182
  29.3 7.5 %collective-permute-done.4.rest_0_ = bf16[512,256]{1,0:T(8,128)(2,1)S(1)} collective-permute-done((bf16[512,256]{1,0:T(8,128)(2,1)S(1)}, bf16[512,256]{1,0:T(8,128)(2,1)S(1)}, u32[]{:S(2)}, u32[]{:S(2)}) %collective-permute-start.4) | collective-permute-done | bytes 262176 | tf_op jit(solution)/shard_map/ppermute | solution.py:45
  36.8 1.4 %collective-permute-start.7 = (bf16[512,256]{1,0:T(8,128)(2,1)S(1)}, bf16[512,256]{1,0:T(8,128)(2,1)S(1)}, u32[]{:S(2)}, u32[]{:S(2)}) collective-permute-start(bf16[512,256]{1,0:T(8,128)(2,1)S(1)} %collective-permute-done.4.rest_0_), channel_id=1, source_target_pairs={{0,4},{1,5},{2,6},{3,7},{4,8},{5,9},{6,10},{7,11},{8,12},{9,13},{1... | collective-permute-start | bytes 786440 | tf_op jit(solution)/shard_map/ppermute | solution.py:45
  38.2 0.7 collective-permute-start.6
  39.0 2.6 %collective-permute-start.5 = (bf16[512,256]{1,0:T(8,128)(2,1)S(1)}, bf16[512,256]{1,0:T(8,128)(2,1)S(1)}, u32[]{:S(2)}, u32[]{:S(2)}) collective-permute-start(bf16[512,256]{1,0:T(8,128)(2,1)S(1)} %collective-permute-done.4.rest_0_), channel_id=1, source_target_pairs={{0,12},{1,13},{2,14},{3,15},{4,0},{5,1},{6,2},{7,3},{8,4},{9,5},{1... | collective-permute-start | bytes 786440 | tf_op jit(solution)/shard_map/ppermute | solution.py:45
  41.6 4.3 %attend.8.rest_1_ = f32[136,2048]{1,0:T(8,128)S(1)} custom-call(bf16[128,2048]{1,0:T(8,128)(2,1)S(1)} %pad_maximum_fusion.q_ref, s32[8,2048]{1,0:T(8,128)S(1)} %broadcast_in_dim.27.low_ref, bf16[512,256]{1,0:T(8,128)(2,1)S(1)} %collective-permute-done.4.rest_0_, ...), custom_call_target="tpu_custom_call", output_to_operand_aliasing={{}: (4, {})} | custom-call | flops 1 | bytes 1 | tf_op jit(solution)/shard_map/attend/pallas_call | solution.py:182
  45.9 2.5 %attend.9.rest_2_ = f32[136,2048]{1,0:T(8,128)S(1)} custom-call(bf16[128,2048]{1,0:T(8,128)(2,1)S(1)} %pad_maximum_fusion.q_ref, s32[8,2048]{1,0:T(8,128)S(1)} %broadcast_in_dim.27.low_ref, bf16[640,256]{1,0:T(8,128)(2,1)S(1)} %collective-permute-done.9.rest_0_, f32[136,2048]{1,0:T(8,128)S(1)} %attend.8.rest_1_), custom_call_target="tpu_custom_call", output_to_operand_aliasing={{}: (3, {})} | custom-call | flops 1 | bytes 1 | tf_op jit(solution)/shard_map/attend/pallas_call | solution.py:182
  48.4 0.0 slice-start.1
  48.4 3.2 %attend.10.rest_1_ = f32[136,2048]{1,0:T(8,128)S(1)} custom-call(bf16[128,2048]{1,0:T(8,128)(2,1)S(1)} %pad_maximum_fusion.q_ref, s32[8,2048]{1,0:T(8,128)S(1)} %broadcast_in_dim.27.low_ref, bf16[640,256]{1,0:T(8,128)(2,1)S(1)} %collective-permute-done.8.rest_0_, ...), custom_call_target="tpu_custom_call", output_to_operand_aliasing={{}: (4, {})} | custom-call | flops 1 | bytes 1 | tf_op jit(solution)/shard_map/attend/pallas_call | solution.py:182
  51.7 2.1 %attend.11.rest_2_ = f32[136,2048]{1,0:T(8,128)S(1)} custom-call(bf16[128,2048]{1,0:T(8,128)(2,1)S(1)} %pad_maximum_fusion.q_ref, s32[8,2048]{1,0:T(8,128)S(1)} %broadcast_in_dim.27.low_ref, bf16[512,256]{1,0:T(8,128)(2,1)S(1)} %collective-permute-done.7.rest_0_, f32[136,2048]{1,0:T(8,128)S(1)} %attend.10.rest_1_), custom_call_target="tpu_custom_call", output_to_operand_aliasing={{}: (3, {})} | custom-call | flops 1 | bytes 1 | tf_op jit(solution)/shard_map/attend/pallas_call | solution.py:182
  53.8 2.2 %attend.13.rest_0_ = f32[136,1024]{1,0:T(8,128)S(1)} custom-call(bf16[128,2048]{1,0:T(8,128)(2,1)S(1)} %pad_maximum_fusion.q_ref, s32[8,2048]{1,0:T(8,128)S(1)} %broadcast_in_dim.27.low_ref, bf16[512,256]{1,0:T(8,128)(2,1)S(1)} %collective-permute-done.5.rest_0_, bf16[512,256]{1,0:T(8,128)(2,1)S(1)} %collective-permute-done.6.rest_1_, ...), custom_call_target="tpu_custom_call" | custom-call | flops 1 | bytes 1 | tf_op jit(solution)/shard_map/attend/pallas_call | solution.py:182
  56.0 0.1 collective-permute-start.15
  56.1 2.0 %attend.12.rest_0_ = f32[136,1024]{1,0:T(8,128)S(1)} custom-call(bf16[128,2048]{1,0:T(8,128)(2,1)S(1)} %pad_maximum_fusion.q_ref, s32[8,2048]{1,0:T(8,128)S(1)} %broadcast_in_dim.27.low_ref, bf16[512,256]{1,0:T(8,128)(2,1)S(1)} %collective-permute-done.5.rest_0_, bf16[512,256]{1,0:T(8,128)(2,1)S(1)} %collective-permute-done.6.rest_1_, ...), custom_call_target="tpu_custom_call" | custom-call | flops 1 | bytes 1 | tf_op jit(solution)/shard_map/attend/pallas_call | solution.py:182
  58.1 0.6 collective-permute-start.12
  58.7 2.5 %project.8 = (bf16[128,1024]{1,0:T(8,128)(2,1)S(1)}, bf16[128,2048]{1,0:T(8,128)(2,1)S(1)}) custom-call(f32[136,1024]{1,0:T(8,128)S(1)} %attend.13.rest_0_, f32[136,1024]{1,0:T(8,128)S(1)} %collective-permute-done.15.rest_1_, bf16[512,8192]{1,0:T(8,128)(2,1)S(1)} %bitcast.14, bf16[512,8192]{1,0:T(8,128)(2,1)} %collective-permute-done.11.rest_3_.rest_2_), custom_call_target="tpu_custom_call" | custom-call | flops 1 | bytes 1 | tf_op jit(solution)/shard_map/project/pallas_call | solution.py:267
  61.2 1.5 %collective-permute-start.16 = (bf16[128,2048]{1,0:T(8,128)(2,1)S(1)}, bf16[128,2048]{1,0:T(8,128)(2,1)S(1)}, u32[]{:S(2)}, u32[]{:S(2)}) collective-permute-start(bf16[128,2048]{1,0:T(8,128)(2,1)S(1)} %get-tuple-element.34), channel_id=1, source_target_pairs={{0,2},{1,3},{2,0},{3,1},{4,6},{5,7},{6,4},{7,5},{8,10},{9,11},{10,... | collective-permute-start | bytes 1572872 | tf_op jit(solution)/shard_map/ppermute | solution.py:45
  62.7 1.8 %project.5 = (bf16[128,1024]{1,0:T(8,128)(2,1)S(1)}, bf16[128,1024]{1,0:T(8,128)(2,1)S(1)}) custom-call(f32[136,1024]{1,0:T(8,128)S(1)} %attend.12.rest_0_, f32[136,1024]{1,0:T(8,128)S(1)} %collective-permute-done.12.rest_1_, bf16[512,8192]{1,0:T(8,128)(2,1)S(1)} %bitcast.14, bf16[512,8192]{1,0:T(8,128)(2,1)} %collective-permute-done.11.rest_3_.rest_2_), custom_call_target="tpu_custom_call" | custom-call | flops 1 | bytes 1 | tf_op jit(solution)/shard_map/project/pallas_call | solution.py:267
  64.5 2.2 %collective-permute-start.14 = (bf16[128,1024]{1,0:T(8,128)(2,1)S(1)}, bf16[128,1024]{1,0:T(8,128)(2,1)S(1)}, u32[]{:S(2)}, u32[]{:S(2)}) collective-permute-start(bf16[128,1024]{1,0:T(8,128)(2,1)S(1)} %get-tuple-element.32), channel_id=1, source_target_pairs={{0,2},{1,3},{2,0},{3,1},{4,6},{5,7},{6,4},{7,5},{8,10},{9,11},{10,... | collective-permute-start | bytes 786440 | tf_op jit(solution)/shard_map/ppermute | solution.py:45
  66.7 1.8 %project.7 = bf16[128,1024]{1,0:T(8,128)(2,1)S(1)} custom-call(bf16[128,1024]{1,0:T(8,128)(2,1)S(1)} %get-tuple-element.31.rest_0_, bf16[512,8192]{1,0:T(8,128)(2,1)S(1)} %bitcast.14, bf16[512,8192]{1,0:T(8,128)(2,1)} %collective-permute-done.11.rest_3_.rest_2_), custom_call_target="tpu_custom_call" | custom-call | flops 1 | bytes 1 | tf_op jit(solution)/shard_map/project/pallas_call | solution.py:267
  68.5 1.5 %collective-permute-start.13 = (bf16[128,1024]{1,0:T(8,128)(2,1)S(1)}, bf16[128,1024]{1,0:T(8,128)(2,1)S(1)}, u32[]{:S(2)}, u32[]{:S(2)}) collective-permute-start(bf16[128,1024]{1,0:T(8,128)(2,1)S(1)} %project.7), channel_id=1, source_target_pairs={{0,2},{1,3},{2,0},{3,1},{4,6},{5,7},{6,4},{7,5},{8,10},{9,11},{10,... | collective-permute-start | bytes 786440 | tf_op jit(solution)/shard_map/ppermute | solution.py:45
  70.0 2.5 %project.6.kept = f32[128,2048]{1,0:T(8,128)S(1)} custom-call(bf16[128,1024]{1,0:T(8,128)(2,1)S(1)} %get-tuple-element.31.rest_0_, bf16[512,8192]{1,0:T(8,128)(2,1)S(1)} %bitcast.14, bf16[512,8192]{1,0:T(8,128)(2,1)} %collective-permute-done.11.rest_3_.rest_2_), custom_call_target="tpu_custom_call" | custom-call | flops 1 | bytes 1 | tf_op jit(solution)/shard_map/project/pallas_call | solution.py:267
  72.4 2.5 %project.9.kept = f32[128,2048]{1,0:T(8,128)S(1)} custom-call(bf16[128,1024]{1,0:T(8,128)(2,1)S(1)} %get-tuple-element.33.rest_0_, bf16[512,8192]{1,0:T(8,128)(2,1)S(1)} %bitcast.14, bf16[512,8192]{1,0:T(8,128)(2,1)} %collective-permute-done.11.rest_3_.rest_2_), custom_call_target="tpu_custom_call" | custom-call | flops 1 | bytes 1 | tf_op jit(solution)/shard_map/project/pallas_call | solution.py:267
  74.9 2.6 %collective-permute-done.16.received = bf16[128,2048]{1,0:T(8,128)(2,1)S(1)} collective-permute-done((bf16[128,2048]{1,0:T(8,128)(2,1)S(1)}, bf16[128,2048]{1,0:T(8,128)(2,1)S(1)}, u32[]{:S(2)}, u32[]{:S(2)}) %collective-permute-start.16) | collective-permute-done | bytes 524320 | tf_op jit(solution)/shard_map/ppermute | solution.py:45
  77.6 1.5 %finish.3.rest_0_ = bf16[256,2048]{1,0:T(8,128)(2,1)} custom-call(f32[128,2048]{1,0:T(8,128)S(1)} %project.9.kept, bf16[128,2048]{1,0:T(8,128)(2,1)S(1)} %collective-permute-done.16.received), custom_call_target="tpu_custom_call" | custom-call | flops 1 | bytes 1 | tf_op jit(solution)/shard_map/finish/pallas_call | solution.py:297
  79.1 4.1 %collective-permute-done.14.received = bf16[128,1024]{1,0:T(8,128)(2,1)S(1)} collective-permute-done((bf16[128,1024]{1,0:T(8,128)(2,1)S(1)}, bf16[128,1024]{1,0:T(8,128)(2,1)S(1)}, u32[]{:S(2)}, u32[]{:S(2)}) %collective-permute-start.14) | collective-permute-done | bytes 262176 | tf_op jit(solution)/shard_map/ppermute | solution.py:45
  83.2 0.8 finish.4.rest_0_
  84.0 3.9 %collective-permute-done.13.received = bf16[128,1024]{1,0:T(8,128)(2,1)S(1)} collective-permute-done((bf16[128,1024]{1,0:T(8,128)(2,1)S(1)}, bf16[128,1024]{1,0:T(8,128)(2,1)S(1)}, u32[]{:S(2)}, u32[]{:S(2)}) %collective-permute-start.13) | collective-permute-done | bytes 262176 | tf_op jit(solution)/shard_map/ppermute | solution.py:45
  87.9 0.8 finish.5
  (28 shorter events, 0.2 us)
Async XLA Ops:
  0.0 12.4 %copy-start = (bf16[256,512]{1,0:T(8,128)(2,1)S(1)}, bf16[256,512]{1,0:T(8,128)(2,1)}, u32[]{:S(2)}) copy-start(bf16[256,512]{1,0:T(8,128)(2,1)} %queries.1) | copy-start | bytes 786436
  2.1 15.6 %copy-start.1 = (s32[8]{0:T(128)S(1)}, s32[8]{0:T(128)}, u32[]{:S(2)}) copy-start(s32[8]{0:T(128)} %param.8) | copy-start | bytes 100
  2.1 11.6 %collective-permute-start.2 = (bf16[256,256]{1,0:T(8,128)(2,1)S(1)}, bf16[256,256]{1,0:T(8,128)(2,1)S(1)}, u32[]{:S(2)}, u32[]{:S(2)}) collective-permute-start(bf16[256,256]{1,0:T(8,128)(2,1)S(1)} %pad_maximum_fusion.3), channel_id=1, source_target_pairs={{12,144},{14,146},{28,160},{30,162},{44,176},{46,178},{60,192},{62... | collective-permute-start | bytes 393224 | tf_op jit(solution)/shard_map/ppermute | solution.py:45
  2.8 11.5 %collective-permute-start.1 = (bf16[256,256]{1,0:T(8,128)(2,1)S(1)}, bf16[256,256]{1,0:T(8,128)(2,1)S(1)}, u32[]{:S(2)}, u32[]{:S(2)}) collective-permute-start(bf16[256,256]{1,0:T(8,128)(2,1)S(1)} %pad_maximum_fusion.3), channel_id=1, source_target_pairs={{0,32},{1,113},{2,34},{3,115},{4,36},{5,117},{6,38},{7,119},{8,40}... | collective-permute-start | bytes 393224 | tf_op jit(solution)/shard_map/ppermute | solution.py:45
  8.6 9.0 %collective-permute-start = (bf16[256,256]{1,0:T(8,128)(2,1)S(1)}, bf16[256,256]{1,0:T(8,128)(2,1)S(1)}, u32[]{:S(2)}, u32[]{:S(2)}) collective-permute-start(bf16[256,256]{1,0:T(8,128)(2,1)S(1)} %pad_maximum_fusion.3), channel_id=1, source_target_pairs={{0,16},{1,129},{2,18},{3,131},{4,20},{5,133},{6,22},{7,135},{8,24}... | collective-permute-start | bytes 393224 | tf_op jit(solution)/shard_map/ppermute | solution.py:45
  13.4 4.2 %collective-permute-start.3 = (bf16[128,1024]{1,0:T(8,128)(2,1)S(1)}, bf16[128,1024]{1,0:T(8,128)(2,1)S(1)}, u32[]{:S(2)}, u32[]{:S(2)}) collective-permute-start(bf16[128,1024]{1,0:T(8,128)(2,1)S(1)} %turn.1), channel_id=1, source_target_pairs={{0,1},{1,0},{2,3},{3,2},{4,5},{5,4},{6,7},{7,6},{8,9},{9,8},{10,11... | collective-permute-start | bytes 786440 | tf_op jit(solution)/shard_map/ppermute | solution.py:45
  17.6 34.0 %collective-permute-start.11 = (bf16[512,8192]{1,0:T(8,128)(2,1)}, bf16[512,8192]{1,0:T(8,128)(2,1)}, u32[]{:S(2)}, u32[]{:S(2)}) collective-permute-start(bf16[512,8192]{1,0:T(8,128)(2,1)} %rest_1_.2), channel_id=1, source_target_pairs={{0,1},{1,0},{2,3},{3,2},{4,5},{5,4},{6,7},{7,6},{8,9},{9,8},{10,11... | collective-permute-start | bytes 25165832 | tf_op jit(solution)/shard_map/ppermute | solution.py:45
  18.0 20.2 %collective-permute-start.10 = (bf16[640,256]{1,0:T(8,128)(2,1)S(1)}, bf16[640,256]{1,0:T(8,128)(2,1)S(1)}, u32[]{:S(2)}, u32[]{:S(2)}) collective-permute-start(bf16[640,256]{1,0:T(8,128)(2,1)S(1)} %pad_maximum_fusion.1), channel_id=1, source_target_pairs={{0,4},{1,5},{2,6},{3,7},{4,8},{5,9},{6,10},{7,11},{8,12},{9,13},{1... | collective-permute-start | bytes 983048 | tf_op jit(solution)/shard_map/ppermute | solution.py:45
  19.3 19.6 %collective-permute-start.9 = (bf16[640,256]{1,0:T(8,128)(2,1)S(1)}, bf16[640,256]{1,0:T(8,128)(2,1)S(1)}, u32[]{:S(2)}, u32[]{:S(2)}) collective-permute-start(bf16[640,256]{1,0:T(8,128)(2,1)S(1)} %pad_maximum_fusion.1), channel_id=1, source_target_pairs={{0,12},{1,13},{2,14},{3,15},{4,0},{5,1},{6,2},{7,3},{8,4},{9,5},{1... | collective-permute-start | bytes 983048 | tf_op jit(solution)/shard_map/ppermute | solution.py:45
  22.2 26.2 %collective-permute-start.8 = (bf16[640,256]{1,0:T(8,128)(2,1)S(1)}, bf16[640,256]{1,0:T(8,128)(2,1)S(1)}, u32[]{:S(2)}, u32[]{:S(2)}) collective-permute-start(bf16[640,256]{1,0:T(8,128)(2,1)S(1)} %pad_maximum_fusion.1), channel_id=1, source_target_pairs={{0,8},{1,9},{2,10},{3,11},{4,12},{5,13},{6,14},{7,15},{8,0},{9,1},... | collective-permute-start | bytes 983048 | tf_op jit(solution)/shard_map/ppermute | solution.py:45
  23.6 13.2 %collective-permute-start.4 = (bf16[512,256]{1,0:T(8,128)(2,1)S(1)}, bf16[512,256]{1,0:T(8,128)(2,1)S(1)}, u32[]{:S(2)}, u32[]{:S(2)}) collective-permute-start(bf16[512,256]{1,0:T(8,128)(2,1)S(1)} %pad_maximum_fusion.2.rest_1_), channel_id=1, source_target_pairs={{0,32},{1,225},{2,34},{3,227},{4,36},{5,229},{6,38},{7,231},{8,40}... | collective-permute-start | bytes 786440 | tf_op jit(solution)/shard_map/ppermute | solution.py:45
  36.8 14.9 %collective-permute-start.7 = (bf16[512,256]{1,0:T(8,128)(2,1)S(1)}, bf16[512,256]{1,0:T(8,128)(2,1)S(1)}, u32[]{:S(2)}, u32[]{:S(2)}) collective-permute-start(bf16[512,256]{1,0:T(8,128)(2,1)S(1)} %collective-permute-done.4.rest_0_), channel_id=1, source_target_pairs={{0,4},{1,5},{2,6},{3,7},{4,8},{5,9},{6,10},{7,11},{8,12},{9,13},{1... | collective-permute-start | bytes 786440 | tf_op jit(solution)/shard_map/ppermute | solution.py:45
  38.2 15.5 %collective-permute-start.6 = (bf16[512,256]{1,0:T(8,128)(2,1)S(1)}, bf16[512,256]{1,0:T(8,128)(2,1)S(1)}, u32[]{:S(2)}, u32[]{:S(2)}) collective-permute-start(bf16[512,256]{1,0:T(8,128)(2,1)S(1)} %collective-permute-done.4.rest_0_), channel_id=1, source_target_pairs={{0,8},{1,9},{2,10},{3,11},{4,12},{5,13},{6,14},{7,15},{8,0},{9,1},... | collective-permute-start | bytes 786440 | tf_op jit(solution)/shard_map/ppermute | solution.py:45
  39.0 14.8 %collective-permute-start.5 = (bf16[512,256]{1,0:T(8,128)(2,1)S(1)}, bf16[512,256]{1,0:T(8,128)(2,1)S(1)}, u32[]{:S(2)}, u32[]{:S(2)}) collective-permute-start(bf16[512,256]{1,0:T(8,128)(2,1)S(1)} %collective-permute-done.4.rest_0_), channel_id=1, source_target_pairs={{0,12},{1,13},{2,14},{3,15},{4,0},{5,1},{6,2},{7,3},{8,4},{9,5},{1... | collective-permute-start | bytes 786440 | tf_op jit(solution)/shard_map/ppermute | solution.py:45
  41.6 17.1 %slice-start = ((s8[8388608]{0:T(1024)(128)(4,1)}), s8[4194304]{0:T(1024)(128)(4,1)S(1)}, s32[]{:S(2)}) async-start(s8[8388608]{0:T(1024)(128)(4,1)} %bitcast.13), calls=%async_computation | async-start | bytes 8388608
  48.4 10.3 %slice-start.1 = ((s8[8388608]{0:T(1024)(128)(4,1)}), s8[4194304]{0:T(1024)(128)(4,1)S(1)}, s32[]{:S(2)}) async-start(s8[8388608]{0:T(1024)(128)(4,1)} %bitcast.13), calls=%async_computation.1 | async-start | bytes 8388608
  56.0 2.7 %collective-permute-start.15 = (f32[136,1024]{1,0:T(8,128)S(1)}, f32[136,1024]{1,0:T(8,128)S(1)}, u32[]{:S(2)}, u32[]{:S(2)}) collective-permute-start(f32[136,1024]{1,0:T(8,128)S(1)} %attend.13.rest_0_), channel_id=1, source_target_pairs={{0,1},{1,0},{2,3},{3,2},{4,5},{5,4},{6,7},{7,6},{8,9},{9,8},{10,11... | collective-permute-start | bytes 1671176 | tf_op jit(solution)/shard_map/ppermute | solution.py:45
  58.1 4.6 %collective-permute-start.12 = (f32[136,1024]{1,0:T(8,128)S(1)}, f32[136,1024]{1,0:T(8,128)S(1)}, u32[]{:S(2)}, u32[]{:S(2)}) collective-permute-start(f32[136,1024]{1,0:T(8,128)S(1)} %attend.12.rest_0_), channel_id=1, source_target_pairs={{0,1},{1,0},{2,3},{3,2},{4,5},{5,4},{6,7},{7,6},{8,9},{9,8},{10,11... | collective-permute-start | bytes 1671176 | tf_op jit(solution)/shard_map/ppermute | solution.py:45
  61.2 16.4 %collective-permute-start.16 = (bf16[128,2048]{1,0:T(8,128)(2,1)S(1)}, bf16[128,2048]{1,0:T(8,128)(2,1)S(1)}, u32[]{:S(2)}, u32[]{:S(2)}) collective-permute-start(bf16[128,2048]{1,0:T(8,128)(2,1)S(1)} %get-tuple-element.34), channel_id=1, source_target_pairs={{0,2},{1,3},{2,0},{3,1},{4,6},{5,7},{6,4},{7,5},{8,10},{9,11},{10,... | collective-permute-start | bytes 1572872 | tf_op jit(solution)/shard_map/ppermute | solution.py:45
  64.5 18.7 %collective-permute-start.14 = (bf16[128,1024]{1,0:T(8,128)(2,1)S(1)}, bf16[128,1024]{1,0:T(8,128)(2,1)S(1)}, u32[]{:S(2)}, u32[]{:S(2)}) collective-permute-start(bf16[128,1024]{1,0:T(8,128)(2,1)S(1)} %get-tuple-element.32), channel_id=1, source_target_pairs={{0,2},{1,3},{2,0},{3,1},{4,6},{5,7},{6,4},{7,5},{8,10},{9,11},{10,... | collective-permute-start | bytes 786440 | tf_op jit(solution)/shard_map/ppermute | solution.py:45
  68.5 19.4 %collective-permute-start.13 = (bf16[128,1024]{1,0:T(8,128)(2,1)S(1)}, bf16[128,1024]{1,0:T(8,128)(2,1)S(1)}, u32[]{:S(2)}, u32[]{:S(2)}) collective-permute-start(bf16[128,1024]{1,0:T(8,128)(2,1)S(1)} %project.7), channel_id=1, source_target_pairs={{0,2},{1,3},{2,0},{3,1},{4,6},{5,7},{6,4},{7,5},{8,10},{9,11},{10,... | collective-permute-start | bytes 786440 | tf_op jit(solution)/shard_map/ppermute | solution.py:45

commit v3 on v1

--- a/solution.py
+++ b/solution.py
@@ -345,7 +345,8 @@
         state = step(refs, kinds, state)
     state, other_weight = lax.optimization_barrier((state, other_weight))
     weights = (out_weight, other_weight)
-    state = step(columns_2[:2], rows_2(1) + rows_2(-1), state)
+    state = step(columns_2[:1], rows_2(1), state)
+    state = step(columns_2[1:2], rows_2(-1), state)
     state = step(columns_2[2:], rows_2(2), state)
 
     theirs = permute(state, other_core)

time: 88.7 us -> 87.9 us (level)
  the two profiles are of different devices: /device:TPU:6 before, /device:TPU:78 now
where the time goes in v3:
time: 87.9 us; the launch traced here: 86.4 us
  starting transfers between devices  36.4 us (41%)
  Pallas kernels  29.8 us (34%)
  waiting for transfers between devices  17.4 us (20%)
  local copies, waits for them, and re-layouts  1.34 us (2%)
  other arithmetic  1.06 us (1%)
    ppermute x17, starting transfers between devices, permute(): return lax.ppermute(x, ('seq', 'tensor'), device_perm(move))  36.4 us
    pallas_call x7, Pallas kernels, attend(): pl.pallas_call(functools.partial(attend_kernel, kinds, state is None), ou...  18.7 us
    ppermute x17, waiting for transfers between devices, permute(): return lax.ppermute(x, ('seq', 'tensor'), device_perm(move))  17.4 us
    pallas_call x3, Pallas kernels, project(): pl.pallas_call(functools.partial(project_kernel, other_side, first, mergi...  7.1 us
    pallas_call x4, Pallas kernels, finish(): pl.pallas_call(finish_kernel, out_shape=jax.ShapeDtypeStruct(kept.shape,...  2.99 us
  transfers between devices with their start and end apart: 17, of which 5 were waited for; matrix products, arithmetic and copies ran while one was open for 0% of the time, Pallas kernels for 29%

profile of v3, /device:TPU:78, one launch (start us, length us, event | category | flops | bytes accessed | tf_op | source)
XLA Modules:
  0.0 86.4 jit_solution(9618257341442708440)
XLA Ops:
  0.1 1.3 %constant_dynamic-slice_fusion.1 = (bf16[256,1,128]{2,1,0:T(2,128)(2,1)S(1)}, bf16[256,1,128]{2,1,0:T(2,128)(2,1)S(1)}) fusion(bf16[256,2,128]{2,1,0:T(2,128)(2,1)} %param.7, s32[]{:T(128)S(6)} %select_n.24, bf16[256,2,128]{2,1,0:T(2,128)(2,1)} %param.6), kind=kLoop, calls=%fused_computation.15 | loop fusion | bytes 262148 | tf_op jit(solution)/shard_map/jit(dynamic_index_in_dim)/dynamic_slice | solution.py:310
  1.4 0.6 subtract_convert_fusion
  2.0 0.1 pad_maximum_fusion.3
  2.1 0.0 copy-start.1
  2.1 0.7 collective-permute-start.2
  2.8 6.4 %collective-permute-start.1 = (bf16[256,256]{1,0:T(8,128)(2,1)S(1)}, bf16[256,256]{1,0:T(8,128)(2,1)S(1)}, u32[]{:S(2)}, u32[]{:S(2)}) collective-permute-start(bf16[256,256]{1,0:T(8,128)(2,1)S(1)} %pad_maximum_fusion.3), channel_id=1, source_target_pairs={{0,32},{1,113},{2,34},{3,115},{4,36},{5,117},{6,38},{7,119},{8,40}... | collective-permute-start | bytes 393224 | tf_op jit(solution)/shard_map/ppermute | solution.py:44
  9.2 2.9 %collective-permute-start = (bf16[256,256]{1,0:T(8,128)(2,1)S(1)}, bf16[256,256]{1,0:T(8,128)(2,1)S(1)}, u32[]{:S(2)}, u32[]{:S(2)}) collective-permute-start(bf16[256,256]{1,0:T(8,128)(2,1)S(1)} %pad_maximum_fusion.3), channel_id=1, source_target_pairs={{0,16},{1,129},{2,18},{3,131},{4,20},{5,133},{6,22},{7,135},{8,24}... | collective-permute-start | bytes 393224 | tf_op jit(solution)/shard_map/ppermute | solution.py:44
  12.1 1.0 %turn.1 = bf16[128,1024]{1,0:T(8,128)(2,1)S(1)} custom-call(bf16[256,512]{1,0:T(8,128)(2,1)S(1)} %copy-done, f32[256,64]{1,0:T(8,128)S(1)} %get-tuple-element.40.cosine, f32[256,64]{1,0:T(8,128)S(1)} %get-tuple-element.39.sine), custom_call_target="tpu_custom_call" | custom-call | flops 1 | bytes 1 | tf_op jit(solution)/shard_map/turn/pallas_call | solution.py:196
  13.1 0.1 collective-permute-start.3
  13.3 2.7 %collective-permute-done = bf16[256,256]{1,0:T(8,128)(2,1)S(1)} collective-permute-done((bf16[256,256]{1,0:T(8,128)(2,1)S(1)}, bf16[256,256]{1,0:T(8,128)(2,1)S(1)}, u32[]{:S(2)}, u32[]{:S(2)}) %collective-permute-start) | collective-permute-done | bytes 131104 | tf_op jit(solution)/shard_map/ppermute | solution.py:44
  16.1 0.0 collective-permute-done.3
  16.1 0.1 collective-permute-start.11
  16.2 0.2 reduce-window.8
  16.4 0.1 select_reduce_fusion
  16.5 1.6 %collective-permute-start.10 = (bf16[640,256]{1,0:T(8,128)(2,1)S(1)}, bf16[640,256]{1,0:T(8,128)(2,1)S(1)}, u32[]{:S(2)}, u32[]{:S(2)}) collective-permute-start(bf16[640,256]{1,0:T(8,128)(2,1)S(1)} %pad_maximum_fusion.1), channel_id=1, source_target_pairs={{0,4},{1,5},{2,6},{3,7},{4,8},{5,9},{6,10},{7,11},{8,12},{9,13},{1... | collective-permute-start | bytes 983048 | tf_op jit(solution)/shard_map/ppermute | solution.py:44
  18.1 0.5 collective-permute-start.9
  18.5 4.6 %collective-permute-start.4 = (bf16[512,256]{1,0:T(8,128)(2,1)S(1)}, bf16[512,256]{1,0:T(8,128)(2,1)S(1)}, u32[]{:S(2)}, u32[]{:S(2)}) collective-permute-start(bf16[512,256]{1,0:T(8,128)(2,1)S(1)} %pad_maximum_fusion.2.rest_1_), channel_id=1, source_target_pairs={{0,32},{1,225},{2,34},{3,227},{4,36},{5,229},{6,38},{7,231},{8,40}... | collective-permute-start | bytes 786440 | tf_op jit(solution)/shard_map/ppermute | solution.py:44
  23.2 2.4 %collective-permute-start.8 = (bf16[640,256]{1,0:T(8,128)(2,1)S(1)}, bf16[640,256]{1,0:T(8,128)(2,1)S(1)}, u32[]{:S(2)}, u32[]{:S(2)}) collective-permute-start(bf16[640,256]{1,0:T(8,128)(2,1)S(1)} %pad_maximum_fusion.1), channel_id=1, source_target_pairs={{0,8},{1,9},{2,10},{3,11},{4,12},{5,13},{6,14},{7,15},{8,0},{9,1},... | collective-permute-start | bytes 983048 | tf_op jit(solution)/shard_map/ppermute | solution.py:44
  25.6 2.2 %attend.7.rest_2_ = f32[136,2048]{1,0:T(8,128)S(1)} custom-call(bf16[128,2048]{1,0:T(8,128)(2,1)S(1)} %pad_maximum_fusion.q_ref, s32[8,2048]{1,0:T(8,128)S(1)} %broadcast_in_dim.25.low_ref, bf16[128,256]{1,0:T(8,128)(2,1)S(1)} %constant_dynamic-slice_fusion.rest_0_, bf16[512,256]{1,0:T(8,128)(2,1)S(1)} %pad_maximum_fusion.2.rest_1_), custom_call_target="tpu_custom_call" | custom-call | flops 1 | bytes 1 | tf_op jit(solution)/shard_map/attend/pallas_call | solution.py:175
  27.8 1.5 %collective-permute-start.7 = (bf16[512,256]{1,0:T(8,128)(2,1)S(1)}, bf16[512,256]{1,0:T(8,128)(2,1)S(1)}, u32[]{:S(2)}, u32[]{:S(2)}) collective-permute-start(bf16[512,256]{1,0:T(8,128)(2,1)S(1)} %collective-permute-done.4.rest_0_), channel_id=1, source_target_pairs={{0,4},{1,5},{2,6},{3,7},{4,8},{5,9},{6,10},{7,11},{8,12},{9,13},{1... | collective-permute-start | bytes 786440 | tf_op jit(solution)/shard_map/ppermute | solution.py:44
  29.4 0.0 collective-permute-done.10.rest_1_
  29.4 0.7 collective-permute-start.6
  30.1 0.0 collective-permute-done.9.rest_0_
  30.1 7.6 %collective-permute-start.5 = (bf16[512,256]{1,0:T(8,128)(2,1)S(1)}, bf16[512,256]{1,0:T(8,128)(2,1)S(1)}, u32[]{:S(2)}, u32[]{:S(2)}) collective-permute-start(bf16[512,256]{1,0:T(8,128)(2,1)S(1)} %collective-permute-done.4.rest_0_), channel_id=1, source_target_pairs={{0,8},{1,9},{2,10},{3,11},{4,12},{5,13},{6,14},{7,15},{8,0},{9,1},... | collective-permute-start | bytes 786440 | tf_op jit(solution)/shard_map/ppermute | solution.py:44
  37.7 4.3 %attend.8.rest_1_ = f32[136,2048]{1,0:T(8,128)S(1)} custom-call(bf16[128,2048]{1,0:T(8,128)(2,1)S(1)} %pad_maximum_fusion.q_ref, s32[8,2048]{1,0:T(8,128)S(1)} %broadcast_in_dim.25.low_ref, bf16[512,256]{1,0:T(8,128)(2,1)S(1)} %collective-permute-done.4.rest_0_, ...), custom_call_target="tpu_custom_call", output_to_operand_aliasing={{}: (4, {})} | custom-call | flops 1 | bytes 1 | tf_op jit(solution)/shard_map/attend/pallas_call | solution.py:175
  42.0 0.0 slice-start
  42.0 2.5 %attend.9.rest_2_ = f32[136,2048]{1,0:T(8,128)S(1)} custom-call(bf16[128,2048]{1,0:T(8,128)(2,1)S(1)} %pad_maximum_fusion.q_ref, s32[8,2048]{1,0:T(8,128)S(1)} %broadcast_in_dim.25.low_ref, bf16[640,256]{1,0:T(8,128)(2,1)S(1)} %collective-permute-done.9.rest_0_, f32[136,2048]{1,0:T(8,128)S(1)} %attend.8.rest_1_), custom_call_target="tpu_custom_call", output_to_operand_aliasing={{}: (3, {})} | custom-call | flops 1 | bytes 1 | tf_op jit(solution)/shard_map/attend/pallas_call | solution.py:175
  44.6 3.2 %attend.10.rest_1_ = f32[136,2048]{1,0:T(8,128)S(1)} custom-call(bf16[128,2048]{1,0:T(8,128)(2,1)S(1)} %pad_maximum_fusion.q_ref, s32[8,2048]{1,0:T(8,128)S(1)} %broadcast_in_dim.25.low_ref, bf16[640,256]{1,0:T(8,128)(2,1)S(1)} %collective-permute-done.8.rest_0_, ...), custom_call_target="tpu_custom_call", output_to_operand_aliasing={{}: (4, {})} | custom-call | flops 1 | bytes 1 | tf_op jit(solution)/shard_map/attend/pallas_call | solution.py:175
  47.8 0.0 slice-start.1
  47.8 2.1 %attend.11.rest_1_ = f32[136,2048]{1,0:T(8,128)S(1)} custom-call(bf16[128,2048]{1,0:T(8,128)(2,1)S(1)} %pad_maximum_fusion.q_ref, s32[8,2048]{1,0:T(8,128)S(1)} %broadcast_in_dim.25.low_ref, bf16[512,256]{1,0:T(8,128)(2,1)S(1)} %collective-permute-done.7.rest_0_, f32[136,2048]{1,0:T(8,128)S(1)} %attend.10.rest_1_), custom_call_target="tpu_custom_call", output_to_operand_aliasing={{}: (3, {})} | custom-call | flops 1 | bytes 1 | tf_op jit(solution)/shard_map/attend/pallas_call | solution.py:175
  49.9 2.3 %attend.12.rest_1_ = f32[136,2048]{1,0:T(8,128)S(1)} custom-call(bf16[128,2048]{1,0:T(8,128)(2,1)S(1)} %pad_maximum_fusion.q_ref, s32[8,2048]{1,0:T(8,128)S(1)} %broadcast_in_dim.25.low_ref, bf16[512,256]{1,0:T(8,128)(2,1)S(1)} %collective-permute-done.6.rest_0_, f32[136,2048]{1,0:T(8,128)S(1)} %attend.11.rest_1_), custom_call_target="tpu_custom_call", output_to_operand_aliasing={{}: (3, {})} | custom-call | flops 1 | bytes 1 | tf_op jit(solution)/shard_map/attend/pallas_call | solution.py:175
  52.2 2.1 %attend.13.rest_0_ = f32[136,2048]{1,0:T(8,128)S(1)} custom-call(bf16[128,2048]{1,0:T(8,128)(2,1)S(1)} %pad_maximum_fusion.q_ref, s32[8,2048]{1,0:T(8,128)S(1)} %broadcast_in_dim.25.low_ref, bf16[512,256]{1,0:T(8,128)(2,1)S(1)} %collective-permute-done.5.rest_0_, f32[136,2048]{1,0:T(8,128)S(1)} %attend.12.rest_1_), custom_call_target="tpu_custom_call", output_to_operand_aliasing={{}: (3, {})} | custom-call | flops 1 | bytes 1 | tf_op jit(solution)/shard_map/attend/pallas_call | solution.py:175
  54.3 0.1 collective-permute-start.12
  54.4 2.7 %collective-permute-done.12.rest_1_ = f32[136,2048]{1,0:T(8,128)S(1)} collective-permute-done((f32[136,2048]{1,0:T(8,128)S(1)}, f32[136,2048]{1,0:T(8,128)S(1)}, u32[]{:S(2)}, u32[]{:S(2)}) %collective-permute-start.12) | collective-permute-done | bytes 1114144 | tf_op jit(solution)/shard_map/ppermute | solution.py:44
  57.2 1.7 %project.3 = (bf16[256,1024]{1,0:T(8,128)(2,1)S(1)}, bf16[256,512]{1,0:T(8,128)(2,1)S(1)}) custom-call(f32[136,2048]{1,0:T(8,128)S(1)} %attend.13.rest_0_, f32[136,2048]{1,0:T(8,128)S(1)} %collective-permute-done.12.rest_1_, bf16[512,8192]{1,0:T(8,128)(2,1)S(1)} %bitcast.14, bf16[512,8192]{1,0:T(8,128)(2,1)} %collective-permute-done.11.rest_3_.rest_2_), custom_call_target="tpu_custom_call" | custom-call | flops 1 | bytes 1 | tf_op jit(solution)/shard_map/project/pallas_call | solution.py:258
  58.8 1.5 %collective-permute-start.16 = (bf16[256,512]{1,0:T(8,128)(2,1)S(1)}, bf16[256,512]{1,0:T(8,128)(2,1)S(1)}, u32[]{:S(2)}, u32[]{:S(2)}) collective-permute-start(bf16[256,512]{1,0:T(8,128)(2,1)S(1)} %get-tuple-element.36), channel_id=1, source_target_pairs={{0,2},{1,3},{2,0},{3,1},{4,6},{5,7},{6,4},{7,5},{8,10},{9,11},{10,... | collective-permute-start | bytes 786440 | tf_op jit(solution)/shard_map/ppermute | solution.py:44
  60.3 2.5 %project.5 = (bf16[256,512]{1,0:T(8,128)(2,1)S(1)}, bf16[256,512]{1,0:T(8,128)(2,1)S(1)}, bf16[256,512]{1,0:T(8,128)(2,1)S(1)}) custom-call(bf16[256,1024]{1,0:T(8,128)(2,1)S(1)} %get-tuple-element.32.rest_0_, bf16[512,8192]{1,0:T(8,128)(2,1)S(1)} %bitcast.14, bf16[512,8192]{1,0:T(8,128)(2,1)} %collective-permute-done.11.rest_3_.rest_2_), custom_call_target="tpu_custom_call" | custom-call | flops 1 | bytes 1 | tf_op jit(solution)/shard_map/project/pallas_call | solution.py:258
  62.8 2.2 %collective-permute-start.15 = (bf16[256,512]{1,0:T(8,128)(2,1)S(1)}, bf16[256,512]{1,0:T(8,128)(2,1)S(1)}, u32[]{:S(2)}, u32[]{:S(2)}) collective-permute-start(bf16[256,512]{1,0:T(8,128)(2,1)S(1)} %get-tuple-element.35), channel_id=1, source_target_pairs={{0,2},{1,3},{2,0},{3,1},{4,6},{5,7},{6,4},{7,5},{8,10},{9,11},{10,... | collective-permute-start | bytes 786440 | tf_op jit(solution)/shard_map/ppermute | solution.py:44
  65.0 1.4 %collective-permute-start.14 = (bf16[256,512]{1,0:T(8,128)(2,1)S(1)}, bf16[256,512]{1,0:T(8,128)(2,1)S(1)}, u32[]{:S(2)}, u32[]{:S(2)}) collective-permute-start(bf16[256,512]{1,0:T(8,128)(2,1)S(1)} %get-tuple-element.34), channel_id=1, source_target_pairs={{0,2},{1,3},{2,0},{3,1},{4,6},{5,7},{6,4},{7,5},{8,10},{9,11},{10,... | collective-permute-start | bytes 786440 | tf_op jit(solution)/shard_map/ppermute | solution.py:44
  66.4 2.1 %collective-permute-start.13 = (bf16[256,512]{1,0:T(8,128)(2,1)S(1)}, bf16[256,512]{1,0:T(8,128)(2,1)S(1)}, u32[]{:S(2)}, u32[]{:S(2)}) collective-permute-start(bf16[256,512]{1,0:T(8,128)(2,1)S(1)} %get-tuple-element.33), channel_id=1, source_target_pairs={{0,2},{1,3},{2,0},{3,1},{4,6},{5,7},{6,4},{7,5},{8,10},{9,11},{10,... | collective-permute-start | bytes 786440 | tf_op jit(solution)/shard_map/ppermute | solution.py:44
  68.6 2.9 %project.4.kept = f32[256,2048]{1,0:T(8,128)S(1)} custom-call(bf16[256,1024]{1,0:T(8,128)(2,1)S(1)} %get-tuple-element.32.rest_0_, bf16[512,8192]{1,0:T(8,128)(2,1)S(1)} %bitcast.14, bf16[512,8192]{1,0:T(8,128)(2,1)} %collective-permute-done.11.rest_3_.rest_2_), custom_call_target="tpu_custom_call" | custom-call | flops 1 | bytes 1 | tf_op jit(solution)/shard_map/project/pallas_call | solution.py:258
  71.5 0.7 finish.4.rest_0_
  72.3 2.9 %collective-permute-done.15.received = bf16[256,512]{1,0:T(8,128)(2,1)S(1)} collective-permute-done((bf16[256,512]{1,0:T(8,128)(2,1)S(1)}, bf16[256,512]{1,0:T(8,128)(2,1)S(1)}, u32[]{:S(2)}, u32[]{:S(2)}) %collective-permute-start.15) | collective-permute-done | bytes 262176 | tf_op jit(solution)/shard_map/ppermute | solution.py:44
  75.2 0.7 finish.5.rest_0_
  75.9 4.9 %collective-permute-done.14.received = bf16[256,512]{1,0:T(8,128)(2,1)S(1)} collective-permute-done((bf16[256,512]{1,0:T(8,128)(2,1)S(1)}, bf16[256,512]{1,0:T(8,128)(2,1)S(1)}, u32[]{:S(2)}, u32[]{:S(2)}) %collective-permute-start.14) | collective-permute-done | bytes 262176 | tf_op jit(solution)/shard_map/ppermute | solution.py:44
  80.8 0.7 finish.6.rest_0_
  81.6 4.1 %collective-permute-done.13.received = bf16[256,512]{1,0:T(8,128)(2,1)S(1)} collective-permute-done((bf16[256,512]{1,0:T(8,128)(2,1)S(1)}, bf16[256,512]{1,0:T(8,128)(2,1)S(1)}, u32[]{:S(2)}, u32[]{:S(2)}) %collective-permute-start.13) | collective-permute-done | bytes 262176 | tf_op jit(solution)/shard_map/ppermute | solution.py:44
  85.6 0.7 finish.7
  (26 shorter events, 0.2 us)
Async XLA Ops:
  0.0 12.1 %copy-start = (bf16[256,512]{1,0:T(8,128)(2,1)S(1)}, bf16[256,512]{1,0:T(8,128)(2,1)}, u32[]{:S(2)}) copy-start(bf16[256,512]{1,0:T(8,128)(2,1)} %queries.1) | copy-start | bytes 786436
  2.1 14.1 %copy-start.1 = (s32[8]{0:T(128)S(1)}, s32[8]{0:T(128)}, u32[]{:S(2)}) copy-start(s32[8]{0:T(128)} %param.8) | copy-start | bytes 100
  2.1 11.2 %collective-permute-start.2 = (bf16[256,256]{1,0:T(8,128)(2,1)S(1)}, bf16[256,256]{1,0:T(8,128)(2,1)S(1)}, u32[]{:S(2)}, u32[]{:S(2)}) collective-permute-start(bf16[256,256]{1,0:T(8,128)(2,1)S(1)} %pad_maximum_fusion.3), channel_id=1, source_target_pairs={{12,144},{14,146},{28,160},{30,162},{44,176},{46,178},{60,192},{62... | collective-permute-start | bytes 393224 | tf_op jit(solution)/shard_map/ppermute | solution.py:44
  2.8 10.5 %collective-permute-start.1 = (bf16[256,256]{1,0:T(8,128)(2,1)S(1)}, bf16[256,256]{1,0:T(8,128)(2,1)S(1)}, u32[]{:S(2)}, u32[]{:S(2)}) collective-permute-start(bf16[256,256]{1,0:T(8,128)(2,1)S(1)} %pad_maximum_fusion.3), channel_id=1, source_target_pairs={{0,32},{1,113},{2,34},{3,115},{4,36},{5,117},{6,38},{7,119},{8,40}... | collective-permute-start | bytes 393224 | tf_op jit(solution)/shard_map/ppermute | solution.py:44
  9.2 6.9 %collective-permute-start = (bf16[256,256]{1,0:T(8,128)(2,1)S(1)}, bf16[256,256]{1,0:T(8,128)(2,1)S(1)}, u32[]{:S(2)}, u32[]{:S(2)}) collective-permute-start(bf16[256,256]{1,0:T(8,128)(2,1)S(1)} %pad_maximum_fusion.3), channel_id=1, source_target_pairs={{0,16},{1,129},{2,18},{3,131},{4,20},{5,133},{6,22},{7,135},{8,24}... | collective-permute-start | bytes 393224 | tf_op jit(solution)/shard_map/ppermute | solution.py:44
  13.1 3.0 %collective-permute-start.3 = (bf16[128,1024]{1,0:T(8,128)(2,1)S(1)}, bf16[128,1024]{1,0:T(8,128)(2,1)S(1)}, u32[]{:S(2)}, u32[]{:S(2)}) collective-permute-start(bf16[128,1024]{1,0:T(8,128)(2,1)S(1)} %turn.1), channel_id=1, source_target_pairs={{0,1},{1,0},{2,3},{3,2},{4,5},{5,4},{6,7},{7,6},{8,9},{9,8},{10,11... | collective-permute-start | bytes 786440 | tf_op jit(solution)/shard_map/ppermute | solution.py:44
  16.1 31.7 %collective-permute-start.11 = (bf16[512,8192]{1,0:T(8,128)(2,1)}, bf16[512,8192]{1,0:T(8,128)(2,1)}, u32[]{:S(2)}, u32[]{:S(2)}) collective-permute-start(bf16[512,8192]{1,0:T(8,128)(2,1)} %rest_1_.1), channel_id=1, source_target_pairs={{0,1},{1,0},{2,3},{3,2},{4,5},{5,4},{6,7},{7,6},{8,9},{9,8},{10,11... | collective-permute-start | bytes 25165832 | tf_op jit(solution)/shard_map/ppermute | solution.py:44
  16.5 12.9 %collective-permute-start.10 = (bf16[640,256]{1,0:T(8,128)(2,1)S(1)}, bf16[640,256]{1,0:T(8,128)(2,1)S(1)}, u32[]{:S(2)}, u32[]{:S(2)}) collective-permute-start(bf16[640,256]{1,0:T(8,128)(2,1)S(1)} %pad_maximum_fusion.1), channel_id=1, source_target_pairs={{0,4},{1,5},{2,6},{3,7},{4,8},{5,9},{6,10},{7,11},{8,12},{9,13},{1... | collective-permute-start | bytes 983048 | tf_op jit(solution)/shard_map/ppermute | solution.py:44
  18.1 12.0 %collective-permute-start.9 = (bf16[640,256]{1,0:T(8,128)(2,1)S(1)}, bf16[640,256]{1,0:T(8,128)(2,1)S(1)}, u32[]{:S(2)}, u32[]{:S(2)}) collective-permute-start(bf16[640,256]{1,0:T(8,128)(2,1)S(1)} %pad_maximum_fusion.1), channel_id=1, source_target_pairs={{0,12},{1,13},{2,14},{3,15},{4,0},{5,1},{6,2},{7,3},{8,4},{9,5},{1... | collective-permute-start | bytes 983048 | tf_op jit(solution)/shard_map/ppermute | solution.py:44
  18.5 9.3 %collective-permute-start.4 = (bf16[512,256]{1,0:T(8,128)(2,1)S(1)}, bf16[512,256]{1,0:T(8,128)(2,1)S(1)}, u32[]{:S(2)}, u32[]{:S(2)}) collective-permute-start(bf16[512,256]{1,0:T(8,128)(2,1)S(1)} %pad_maximum_fusion.2.rest_1_), channel_id=1, source_target_pairs={{0,32},{1,225},{2,34},{3,227},{4,36},{5,229},{6,38},{7,231},{8,40}... | collective-permute-start | bytes 786440 | tf_op jit(solution)/shard_map/ppermute | solution.py:44
  23.2 21.4 %collective-permute-start.8 = (bf16[640,256]{1,0:T(8,128)(2,1)S(1)}, bf16[640,256]{1,0:T(8,128)(2,1)S(1)}, u32[]{:S(2)}, u32[]{:S(2)}) collective-permute-start(bf16[640,256]{1,0:T(8,128)(2,1)S(1)} %pad_maximum_fusion.1), channel_id=1, source_target_pairs={{0,8},{1,9},{2,10},{3,11},{4,12},{5,13},{6,14},{7,15},{8,0},{9,1},... | collective-permute-start | bytes 983048 | tf_op jit(solution)/shard_map/ppermute | solution.py:44
  27.8 20.0 %collective-permute-start.7 = (bf16[512,256]{1,0:T(8,128)(2,1)S(1)}, bf16[512,256]{1,0:T(8,128)(2,1)S(1)}, u32[]{:S(2)}, u32[]{:S(2)}) collective-permute-start(bf16[512,256]{1,0:T(8,128)(2,1)S(1)} %collective-permute-done.4.rest_0_), channel_id=1, source_target_pairs={{0,4},{1,5},{2,6},{3,7},{4,8},{5,9},{6,10},{7,11},{8,12},{9,13},{1... | collective-permute-start | bytes 786440 | tf_op jit(solution)/shard_map/ppermute | solution.py:44
  29.4 20.5 %collective-permute-start.6 = (bf16[512,256]{1,0:T(8,128)(2,1)S(1)}, bf16[512,256]{1,0:T(8,128)(2,1)S(1)}, u32[]{:S(2)}, u32[]{:S(2)}) collective-permute-start(bf16[512,256]{1,0:T(8,128)(2,1)S(1)} %collective-permute-done.4.rest_0_), channel_id=1, source_target_pairs={{0,12},{1,13},{2,14},{3,15},{4,0},{5,1},{6,2},{7,3},{8,4},{9,5},{1... | collective-permute-start | bytes 786440 | tf_op jit(solution)/shard_map/ppermute | solution.py:44
  30.1 22.1 %collective-permute-start.5 = (bf16[512,256]{1,0:T(8,128)(2,1)S(1)}, bf16[512,256]{1,0:T(8,128)(2,1)S(1)}, u32[]{:S(2)}, u32[]{:S(2)}) collective-permute-start(bf16[512,256]{1,0:T(8,128)(2,1)S(1)} %collective-permute-done.4.rest_0_), channel_id=1, source_target_pairs={{0,8},{1,9},{2,10},{3,11},{4,12},{5,13},{6,14},{7,15},{8,0},{9,1},... | collective-permute-start | bytes 786440 | tf_op jit(solution)/shard_map/ppermute | solution.py:44
  42.0 15.1 %slice-start = ((s8[8388608]{0:T(1024)(128)(4,1)}), s8[4194304]{0:T(1024)(128)(4,1)S(1)}, s32[]{:S(2)}) async-start(s8[8388608]{0:T(1024)(128)(4,1)} %bitcast.13), calls=%async_computation | async-start | bytes 8388608
  47.8 9.4 %slice-start.1 = ((s8[8388608]{0:T(1024)(128)(4,1)}), s8[4194304]{0:T(1024)(128)(4,1)S(1)}, s32[]{:S(2)}) async-start(s8[8388608]{0:T(1024)(128)(4,1)} %bitcast.13), calls=%async_computation.1 | async-start | bytes 8388608
  54.3 2.8 %collective-permute-start.12 = (f32[136,2048]{1,0:T(8,128)S(1)}, f32[136,2048]{1,0:T(8,128)S(1)}, u32[]{:S(2)}, u32[]{:S(2)}) collective-permute-start(f32[136,2048]{1,0:T(8,128)S(1)} %attend.13.rest_0_), channel_id=1, source_target_pairs={{0,1},{1,0},{2,3},{3,2},{4,5},{5,4},{6,7},{7,6},{8,9},{9,8},{10,11... | collective-permute-start | bytes 3342344 | tf_op jit(solution)/shard_map/ppermute | solution.py:44
  58.8 12.7 %collective-permute-start.16 = (bf16[256,512]{1,0:T(8,128)(2,1)S(1)}, bf16[256,512]{1,0:T(8,128)(2,1)S(1)}, u32[]{:S(2)}, u32[]{:S(2)}) collective-permute-start(bf16[256,512]{1,0:T(8,128)(2,1)S(1)} %get-tuple-element.36), channel_id=1, source_target_pairs={{0,2},{1,3},{2,0},{3,1},{4,6},{5,7},{6,4},{7,5},{8,10},{9,11},{10,... | collective-permute-start | bytes 786440 | tf_op jit(solution)/shard_map/ppermute | solution.py:44
  62.8 12.4 %collective-permute-start.15 = (bf16[256,512]{1,0:T(8,128)(2,1)S(1)}, bf16[256,512]{1,0:T(8,128)(2,1)S(1)}, u32[]{:S(2)}, u32[]{:S(2)}) collective-permute-start(bf16[256,512]{1,0:T(8,128)(2,1)S(1)} %get-tuple-element.35), channel_id=1, source_target_pairs={{0,2},{1,3},{2,0},{3,1},{4,6},{5,7},{6,4},{7,5},{8,10},{9,11},{10,... | collective-permute-start | bytes 786440 | tf_op jit(solution)/shard_map/ppermute | solution.py:44
  65.0 15.8 %collective-permute-start.14 = (bf16[256,512]{1,0:T(8,128)(2,1)S(1)}, bf16[256,512]{1,0:T(8,128)(2,1)S(1)}, u32[]{:S(2)}, u32[]{:S(2)}) collective-permute-start(bf16[256,512]{1,0:T(8,128)(2,1)S(1)} %get-tuple-element.34), channel_id=1, source_target_pairs={{0,2},{1,3},{2,0},{3,1},{4,6},{5,7},{6,4},{7,5},{8,10},{9,11},{10,... | collective-permute-start | bytes 786440 | tf_op jit(solution)/shard_map/ppermute | solution.py:44
  66.4 19.2 %collective-permute-start.13 = (bf16[256,512]{1,0:T(8,128)(2,1)S(1)}, bf16[256,512]{1,0:T(8,128)(2,1)S(1)}, u32[]{:S(2)}, u32[]{:S(2)}) collective-permute-start(bf16[256,512]{1,0:T(8,128)(2,1)S(1)} %get-tuple-element.33), channel_id=1, source_target_pairs={{0,2},{1,3},{2,0},{3,1},{4,6},{5,7},{6,4},{7,5},{8,10},{9,11},{10,... | collective-permute-start | bytes 786440 | tf_op jit(solution)/shard_map/ppermute | solution.py:44

commit v4 on v3

--- a/solution.py
+++ b/solution.py
@@ -336,10 +336,9 @@
     rows_2 = lambda shift: [(3, shift), (4, shift)]
     group_2, state = lax.optimization_barrier((group_2, state))
     columns_2 = [permute(group_2, in_row(shift)) for shift in shifts]
+    state = step([group_2], rows_2(0), state)
     for shift, keys in zip(shifts, columns_1):
         refs, kinds = [keys], [("half", shift), (1, shift), (2, shift)]
-        if shift == 1:
-            refs, kinds = [group_2] + refs, rows_2(0) + kinds
         if shift == 2:
             refs, kinds = refs + [far], kinds + [("far", 0)]
         state = step(refs, kinds, state)

time: 87.9 us -> 89.6 us (1.019)
  the two profiles are of different devices: /device:TPU:78 before, /device:TPU:6 now
where the time goes in v4:
time: 89.6 us; the launch traced here: 88 us
  starting transfers between devices  30.4 us (34%)
  Pallas kernels  30.3 us (34%)
  waiting for transfers between devices  24.5 us (27%)
  local copies, waits for them, and re-layouts  1.34 us (1%)
  other arithmetic  1.06 us (1%)
    ppermute x17, starting transfers between devices, permute(): return lax.ppermute(x, ('seq', 'tensor'), device_perm(move))  30.4 us
    ppermute x17, waiting for transfers between devices, permute(): return lax.ppermute(x, ('seq', 'tensor'), device_perm(move))  24.5 us
    pallas_call x8, Pallas kernels, attend(): pl.pallas_call(functools.partial(attend_kernel, kinds, state is None), ou...  19.1 us
    pallas_call x3, Pallas kernels, project(): pl.pallas_call(functools.partial(project_kernel, other_side, first, mergi...  7.1 us
    pallas_call x4, Pallas kernels, finish(): pl.pallas_call(finish_kernel, out_shape=jax.ShapeDtypeStruct(kept.shape,...  2.99 us
  transfers between devices with their start and end apart: 17, of which 7 were waited for; matrix products, arithmetic and copies ran while one was open for 0% of the time, Pallas kernels for 29%

profile of v4, /device:TPU:6, one launch (start us, length us, event | category | flops | bytes accessed | tf_op | source)
XLA Modules:
  0.0 88.0 jit_solution(11723662152636626768)
XLA Ops:
  0.1 1.3 %constant_dynamic-slice_fusion.1 = (bf16[256,1,128]{2,1,0:T(2,128)(2,1)S(1)}, bf16[256,1,128]{2,1,0:T(2,128)(2,1)S(1)}) fusion(bf16[256,2,128]{2,1,0:T(2,128)(2,1)} %param.7, s32[]{:T(128)S(6)} %select_n.24, bf16[256,2,128]{2,1,0:T(2,128)(2,1)} %param.6), kind=kLoop, calls=%fused_computation.15 | loop fusion | bytes 262148 | tf_op jit(solution)/shard_map/jit(dynamic_index_in_dim)/dynamic_slice | solution.py:310
  1.4 0.6 subtract_convert_fusion
  2.0 0.1 pad_maximum_fusion.3
  2.1 0.0 copy-start.1
  2.1 0.7 collective-permute-start.2
  2.8 5.8 %collective-permute-start.1 = (bf16[256,256]{1,0:T(8,128)(2,1)S(1)}, bf16[256,256]{1,0:T(8,128)(2,1)S(1)}, u32[]{:S(2)}, u32[]{:S(2)}) collective-permute-start(bf16[256,256]{1,0:T(8,128)(2,1)S(1)} %pad_maximum_fusion.3), channel_id=1, source_target_pairs={{0,32},{1,113},{2,34},{3,115},{4,36},{5,117},{6,38},{7,119},{8,40}... | collective-permute-start | bytes 393224 | tf_op jit(solution)/shard_map/ppermute | solution.py:44
  8.6 3.8 %collective-permute-start = (bf16[256,256]{1,0:T(8,128)(2,1)S(1)}, bf16[256,256]{1,0:T(8,128)(2,1)S(1)}, u32[]{:S(2)}, u32[]{:S(2)}) collective-permute-start(bf16[256,256]{1,0:T(8,128)(2,1)S(1)} %pad_maximum_fusion.3), channel_id=1, source_target_pairs={{0,16},{1,129},{2,18},{3,131},{4,20},{5,133},{6,22},{7,135},{8,24}... | collective-permute-start | bytes 393224 | tf_op jit(solution)/shard_map/ppermute | solution.py:44
  12.4 1.0 %turn.1 = bf16[128,1024]{1,0:T(8,128)(2,1)S(1)} custom-call(bf16[256,512]{1,0:T(8,128)(2,1)S(1)} %copy-done, f32[256,64]{1,0:T(8,128)S(1)} %get-tuple-element.40.cosine, f32[256,64]{1,0:T(8,128)S(1)} %get-tuple-element.39.sine), custom_call_target="tpu_custom_call" | custom-call | flops 1 | bytes 1 | tf_op jit(solution)/shard_map/turn/pallas_call | solution.py:196
  13.4 0.2 collective-permute-start.3
  13.7 0.0 collective-permute-done.2.rest_1_
  13.7 0.6 collective-permute-done.1
  14.3 3.3 %collective-permute-done = bf16[256,256]{1,0:T(8,128)(2,1)S(1)} collective-permute-done((bf16[256,256]{1,0:T(8,128)(2,1)S(1)}, bf16[256,256]{1,0:T(8,128)(2,1)S(1)}, u32[]{:S(2)}, u32[]{:S(2)}) %collective-permute-start) | collective-permute-done | bytes 131104 | tf_op jit(solution)/shard_map/ppermute | solution.py:44
  17.6 0.1 collective-permute-start.11
  17.7 0.2 reduce-window.8
  17.9 0.1 select_reduce_fusion
  18.0 1.3 %collective-permute-start.10 = (bf16[640,256]{1,0:T(8,128)(2,1)S(1)}, bf16[640,256]{1,0:T(8,128)(2,1)S(1)}, u32[]{:S(2)}, u32[]{:S(2)}) collective-permute-start(bf16[640,256]{1,0:T(8,128)(2,1)S(1)} %pad_maximum_fusion.1), channel_id=1, source_target_pairs={{0,4},{1,5},{2,6},{3,7},{4,8},{5,9},{6,10},{7,11},{8,12},{9,13},{1... | collective-permute-start | bytes 983048 | tf_op jit(solution)/shard_map/ppermute | solution.py:44
  19.3 2.9 %collective-permute-start.9 = (bf16[640,256]{1,0:T(8,128)(2,1)S(1)}, bf16[640,256]{1,0:T(8,128)(2,1)S(1)}, u32[]{:S(2)}, u32[]{:S(2)}) collective-permute-start(bf16[640,256]{1,0:T(8,128)(2,1)S(1)} %pad_maximum_fusion.1), channel_id=1, source_target_pairs={{0,12},{1,13},{2,14},{3,15},{4,0},{5,1},{6,2},{7,3},{8,4},{9,5},{1... | collective-permute-start | bytes 983048 | tf_op jit(solution)/shard_map/ppermute | solution.py:44
  22.2 3.4 %collective-permute-start.4 = (bf16[512,256]{1,0:T(8,128)(2,1)S(1)}, bf16[512,256]{1,0:T(8,128)(2,1)S(1)}, u32[]{:S(2)}, u32[]{:S(2)}) collective-permute-start(bf16[512,256]{1,0:T(8,128)(2,1)S(1)} %pad_maximum_fusion.2.rest_1_), channel_id=1, source_target_pairs={{0,32},{1,225},{2,34},{3,227},{4,36},{5,229},{6,38},{7,231},{8,40}... | collective-permute-start | bytes 786440 | tf_op jit(solution)/shard_map/ppermute | solution.py:44
  25.6 1.4 %collective-permute-start.8 = (bf16[640,256]{1,0:T(8,128)(2,1)S(1)}, bf16[640,256]{1,0:T(8,128)(2,1)S(1)}, u32[]{:S(2)}, u32[]{:S(2)}) collective-permute-start(bf16[640,256]{1,0:T(8,128)(2,1)S(1)} %pad_maximum_fusion.1), channel_id=1, source_target_pairs={{0,8},{1,9},{2,10},{3,11},{4,12},{5,13},{6,14},{7,15},{8,0},{9,1},... | collective-permute-start | bytes 983048 | tf_op jit(solution)/shard_map/ppermute | solution.py:44
  27.1 2.2 %attend.8.rest_1_ = f32[136,2048]{1,0:T(8,128)S(1)} custom-call(bf16[128,2048]{1,0:T(8,128)(2,1)S(1)} %pad_maximum_fusion.q_ref, s32[8,2048]{1,0:T(8,128)S(1)} %broadcast_in_dim.25.low_ref, bf16[128,256]{1,0:T(8,128)(2,1)S(1)} %constant_dynamic-slice_fusion.rest_0_, bf16[512,256]{1,0:T(8,128)(2,1)S(1)} %pad_maximum_fusion.2.rest_1_), custom_call_target="tpu_custom_call" | custom-call | flops 1 | bytes 1 | tf_op jit(solution)/shard_map/attend/pallas_call | solution.py:175
  29.3 6.0 %collective-permute-done.4.rest_0_ = bf16[512,256]{1,0:T(8,128)(2,1)S(1)} collective-permute-done((bf16[512,256]{1,0:T(8,128)(2,1)S(1)}, bf16[512,256]{1,0:T(8,128)(2,1)S(1)}, u32[]{:S(2)}, u32[]{:S(2)}) %collective-permute-start.4) | collective-permute-done | bytes 262176 | tf_op jit(solution)/shard_map/ppermute | solution.py:44
  35.4 3.2 %collective-permute-start.6 = (bf16[512,256]{1,0:T(8,128)(2,1)S(1)}, bf16[512,256]{1,0:T(8,128)(2,1)S(1)}, u32[]{:S(2)}, u32[]{:S(2)}) collective-permute-start(bf16[512,256]{1,0:T(8,128)(2,1)S(1)} %collective-permute-done.4.rest_0_), channel_id=1, source_target_pairs={{0,12},{1,13},{2,14},{3,15},{4,0},{5,1},{6,2},{7,3},{8,4},{9,5},{1... | collective-permute-start | bytes 786440 | tf_op jit(solution)/shard_map/ppermute | solution.py:44
  38.6 0.3 collective-permute-start.5
  38.9 2.1 %attend.9.rest_1_ = f32[136,2048]{1,0:T(8,128)S(1)} custom-call(bf16[128,2048]{1,0:T(8,128)(2,1)S(1)} %pad_maximum_fusion.q_ref, s32[8,2048]{1,0:T(8,128)S(1)} %broadcast_in_dim.25.low_ref, bf16[512,256]{1,0:T(8,128)(2,1)S(1)} %collective-permute-done.4.rest_0_, f32[136,2048]{1,0:T(8,128)S(1)} %attend.8.rest_1_), custom_call_target="tpu_custom_call", output_to_operand_aliasing={{}: (3, {})} | custom-call | flops 1 | bytes 1 | tf_op jit(solution)/shard_map/attend/pallas_call | solution.py:175
  40.9 2.7 %attend.10.rest_1_ = f32[136,2048]{1,0:T(8,128)S(1)} custom-call(bf16[128,2048]{1,0:T(8,128)(2,1)S(1)} %pad_maximum_fusion.q_ref, s32[8,2048]{1,0:T(8,128)S(1)} %broadcast_in_dim.25.low_ref, bf16[640,256]{1,0:T(8,128)(2,1)S(1)} %collective-permute-done.10.rest_0_, f32[136,2048]{1,0:T(8,128)S(1)} %attend.9.rest_1_), custom_call_target="tpu_custom_call", output_to_operand_aliasing={{}: (3, {})} | custom-call | flops 1 | bytes 1 | tf_op jit(solution)/shard_map/attend/pallas_call | solution.py:175
  43.6 0.0 slice-start
  43.6 2.5 %attend.11.rest_2_ = f32[136,2048]{1,0:T(8,128)S(1)} custom-call(bf16[128,2048]{1,0:T(8,128)(2,1)S(1)} %pad_maximum_fusion.q_ref, s32[8,2048]{1,0:T(8,128)S(1)} %broadcast_in_dim.25.low_ref, bf16[640,256]{1,0:T(8,128)(2,1)S(1)} %collective-permute-done.9.rest_0_, f32[136,2048]{1,0:T(8,128)S(1)} %attend.10.rest_1_), custom_call_target="tpu_custom_call", output_to_operand_aliasing={{}: (3, {})} | custom-call | flops 1 | bytes 1 | tf_op jit(solution)/shard_map/attend/pallas_call | solution.py:175
  46.2 3.2 %attend.12.rest_1_ = f32[136,2048]{1,0:T(8,128)S(1)} custom-call(bf16[128,2048]{1,0:T(8,128)(2,1)S(1)} %pad_maximum_fusion.q_ref, s32[8,2048]{1,0:T(8,128)S(1)} %broadcast_in_dim.25.low_ref, bf16[640,256]{1,0:T(8,128)(2,1)S(1)} %collective-permute-done.8.rest_0_, ...), custom_call_target="tpu_custom_call", output_to_operand_aliasing={{}: (4, {})} | custom-call | flops 1 | bytes 1 | tf_op jit(solution)/shard_map/attend/pallas_call | solution.py:175
  49.4 0.0 slice-start.1
  49.4 2.1 %attend.13.rest_1_ = f32[136,2048]{1,0:T(8,128)S(1)} custom-call(bf16[128,2048]{1,0:T(8,128)(2,1)S(1)} %pad_maximum_fusion.q_ref, s32[8,2048]{1,0:T(8,128)S(1)} %broadcast_in_dim.25.low_ref, bf16[512,256]{1,0:T(8,128)(2,1)S(1)} %collective-permute-done.7.rest_0_, f32[136,2048]{1,0:T(8,128)S(1)} %attend.12.rest_1_), custom_call_target="tpu_custom_call", output_to_operand_aliasing={{}: (3, {})} | custom-call | flops 1 | bytes 1 | tf_op jit(solution)/shard_map/attend/pallas_call | solution.py:175
  51.5 2.1 %attend.14.rest_1_ = f32[136,2048]{1,0:T(8,128)S(1)} custom-call(bf16[128,2048]{1,0:T(8,128)(2,1)S(1)} %pad_maximum_fusion.q_ref, s32[8,2048]{1,0:T(8,128)S(1)} %broadcast_in_dim.25.low_ref, bf16[512,256]{1,0:T(8,128)(2,1)S(1)} %collective-permute-done.6.rest_0_, f32[136,2048]{1,0:T(8,128)S(1)} %attend.13.rest_1_), custom_call_target="tpu_custom_call", output_to_operand_aliasing={{}: (3, {})} | custom-call | flops 1 | bytes 1 | tf_op jit(solution)/shard_map/attend/pallas_call | solution.py:175
  53.6 2.3 %attend.15.rest_0_ = f32[136,2048]{1,0:T(8,128)S(1)} custom-call(bf16[128,2048]{1,0:T(8,128)(2,1)S(1)} %pad_maximum_fusion.q_ref, s32[8,2048]{1,0:T(8,128)S(1)} %broadcast_in_dim.25.low_ref, bf16[512,256]{1,0:T(8,128)(2,1)S(1)} %collective-permute-done.5.rest_0_, f32[136,2048]{1,0:T(8,128)S(1)} %attend.14.rest_1_), custom_call_target="tpu_custom_call", output_to_operand_aliasing={{}: (3, {})} | custom-call | flops 1 | bytes 1 | tf_op jit(solution)/shard_map/attend/pallas_call | solution.py:175
  55.9 0.1 collective-permute-start.12
  56.0 2.7 %collective-permute-done.12.rest_1_ = f32[136,2048]{1,0:T(8,128)S(1)} collective-permute-done((f32[136,2048]{1,0:T(8,128)S(1)}, f32[136,2048]{1,0:T(8,128)S(1)}, u32[]{:S(2)}, u32[]{:S(2)}) %collective-permute-start.12) | collective-permute-done | bytes 1114144 | tf_op jit(solution)/shard_map/ppermute | solution.py:44
  58.8 1.7 %project.3 = (bf16[256,1024]{1,0:T(8,128)(2,1)S(1)}, bf16[256,512]{1,0:T(8,128)(2,1)S(1)}) custom-call(f32[136,2048]{1,0:T(8,128)S(1)} %attend.15.rest_0_, f32[136,2048]{1,0:T(8,128)S(1)} %collective-permute-done.12.rest_1_, bf16[512,8192]{1,0:T(8,128)(2,1)S(1)} %bitcast.14, bf16[512,8192]{1,0:T(8,128)(2,1)} %collective-permute-done.11.rest_3_.rest_2_), custom_call_target="tpu_custom_call" | custom-call | flops 1 | bytes 1 | tf_op jit(solution)/shard_map/project/pallas_call | solution.py:258
  60.4 1.5 %collective-permute-start.16 = (bf16[256,512]{1,0:T(8,128)(2,1)S(1)}, bf16[256,512]{1,0:T(8,128)(2,1)S(1)}, u32[]{:S(2)}, u32[]{:S(2)}) collective-permute-start(bf16[256,512]{1,0:T(8,128)(2,1)S(1)} %get-tuple-element.36), channel_id=1, source_target_pairs={{0,2},{1,3},{2,0},{3,1},{4,6},{5,7},{6,4},{7,5},{8,10},{9,11},{10,... | collective-permute-start | bytes 786440 | tf_op jit(solution)/shard_map/ppermute | solution.py:44
  61.9 2.5 %project.5 = (bf16[256,512]{1,0:T(8,128)(2,1)S(1)}, bf16[256,512]{1,0:T(8,128)(2,1)S(1)}, bf16[256,512]{1,0:T(8,128)(2,1)S(1)}) custom-call(bf16[256,1024]{1,0:T(8,128)(2,1)S(1)} %get-tuple-element.32.rest_0_, bf16[512,8192]{1,0:T(8,128)(2,1)S(1)} %bitcast.14, bf16[512,8192]{1,0:T(8,128)(2,1)} %collective-permute-done.11.rest_3_.rest_2_), custom_call_target="tpu_custom_call" | custom-call | flops 1 | bytes 1 | tf_op jit(solution)/shard_map/project/pallas_call | solution.py:258
  64.4 2.2 %collective-permute-start.15 = (bf16[256,512]{1,0:T(8,128)(2,1)S(1)}, bf16[256,512]{1,0:T(8,128)(2,1)S(1)}, u32[]{:S(2)}, u32[]{:S(2)}) collective-permute-start(bf16[256,512]{1,0:T(8,128)(2,1)S(1)} %get-tuple-element.35), channel_id=1, source_target_pairs={{0,2},{1,3},{2,0},{3,1},{4,6},{5,7},{6,4},{7,5},{8,10},{9,11},{10,... | collective-permute-start | bytes 786440 | tf_op jit(solution)/shard_map/ppermute | solution.py:44
  66.6 1.4 %collective-permute-start.14 = (bf16[256,512]{1,0:T(8,128)(2,1)S(1)}, bf16[256,512]{1,0:T(8,128)(2,1)S(1)}, u32[]{:S(2)}, u32[]{:S(2)}) collective-permute-start(bf16[256,512]{1,0:T(8,128)(2,1)S(1)} %get-tuple-element.34), channel_id=1, source_target_pairs={{0,2},{1,3},{2,0},{3,1},{4,6},{5,7},{6,4},{7,5},{8,10},{9,11},{10,... | collective-permute-start | bytes 786440 | tf_op jit(solution)/shard_map/ppermute | solution.py:44
  68.0 2.1 %collective-permute-start.13 = (bf16[256,512]{1,0:T(8,128)(2,1)S(1)}, bf16[256,512]{1,0:T(8,128)(2,1)S(1)}, u32[]{:S(2)}, u32[]{:S(2)}) collective-permute-start(bf16[256,512]{1,0:T(8,128)(2,1)S(1)} %get-tuple-element.33), channel_id=1, source_target_pairs={{0,2},{1,3},{2,0},{3,1},{4,6},{5,7},{6,4},{7,5},{8,10},{9,11},{10,... | collective-permute-start | bytes 786440 | tf_op jit(solution)/shard_map/ppermute | solution.py:44
  70.2 2.9 %project.4.kept = f32[256,2048]{1,0:T(8,128)S(1)} custom-call(bf16[256,1024]{1,0:T(8,128)(2,1)S(1)} %get-tuple-element.32.rest_0_, bf16[512,8192]{1,0:T(8,128)(2,1)S(1)} %bitcast.14, bf16[512,8192]{1,0:T(8,128)(2,1)} %collective-permute-done.11.rest_3_.rest_2_), custom_call_target="tpu_custom_call" | custom-call | flops 1 | bytes 1 | tf_op jit(solution)/shard_map/project/pallas_call | solution.py:258
  73.1 0.7 finish.4.rest_0_
  73.9 2.9 %collective-permute-done.15.received = bf16[256,512]{1,0:T(8,128)(2,1)S(1)} collective-permute-done((bf16[256,512]{1,0:T(8,128)(2,1)S(1)}, bf16[256,512]{1,0:T(8,128)(2,1)S(1)}, u32[]{:S(2)}, u32[]{:S(2)}) %collective-permute-start.15) | collective-permute-done | bytes 262176 | tf_op jit(solution)/shard_map/ppermute | solution.py:44
  76.8 0.7 finish.5.rest_0_
  77.5 4.9 %collective-permute-done.14.received = bf16[256,512]{1,0:T(8,128)(2,1)S(1)} collective-permute-done((bf16[256,512]{1,0:T(8,128)(2,1)S(1)}, bf16[256,512]{1,0:T(8,128)(2,1)S(1)}, u32[]{:S(2)}, u32[]{:S(2)}) %collective-permute-start.14) | collective-permute-done | bytes 262176 | tf_op jit(solution)/shard_map/ppermute | solution.py:44
  82.4 0.7 finish.6.rest_0_
  83.2 4.1 %collective-permute-done.13.received = bf16[256,512]{1,0:T(8,128)(2,1)S(1)} collective-permute-done((bf16[256,512]{1,0:T(8,128)(2,1)S(1)}, bf16[256,512]{1,0:T(8,128)(2,1)S(1)}, u32[]{:S(2)}, u32[]{:S(2)}) %collective-permute-start.13) | collective-permute-done | bytes 262176 | tf_op jit(solution)/shard_map/ppermute | solution.py:44
  87.2 0.7 finish.7
  (27 shorter events, 0.2 us)
Async XLA Ops:
  0.0 12.4 %copy-start = (bf16[256,512]{1,0:T(8,128)(2,1)S(1)}, bf16[256,512]{1,0:T(8,128)(2,1)}, u32[]{:S(2)}) copy-start(bf16[256,512]{1,0:T(8,128)(2,1)} %queries.1) | copy-start | bytes 786436
  2.1 15.6 %copy-start.1 = (s32[8]{0:T(128)S(1)}, s32[8]{0:T(128)}, u32[]{:S(2)}) copy-start(s32[8]{0:T(128)} %param.8) | copy-start | bytes 100
  2.1 11.6 %collective-permute-start.2 = (bf16[256,256]{1,0:T(8,128)(2,1)S(1)}, bf16[256,256]{1,0:T(8,128)(2,1)S(1)}, u32[]{:S(2)}, u32[]{:S(2)}) collective-permute-start(bf16[256,256]{1,0:T(8,128)(2,1)S(1)} %pad_maximum_fusion.3), channel_id=1, source_target_pairs={{12,144},{14,146},{28,160},{30,162},{44,176},{46,178},{60,192},{62... | collective-permute-start | bytes 393224 | tf_op jit(solution)/shard_map/ppermute | solution.py:44
  2.8 11.5 %collective-permute-start.1 = (bf16[256,256]{1,0:T(8,128)(2,1)S(1)}, bf16[256,256]{1,0:T(8,128)(2,1)S(1)}, u32[]{:S(2)}, u32[]{:S(2)}) collective-permute-start(bf16[256,256]{1,0:T(8,128)(2,1)S(1)} %pad_maximum_fusion.3), channel_id=1, source_target_pairs={{0,32},{1,113},{2,34},{3,115},{4,36},{5,117},{6,38},{7,119},{8,40}... | collective-permute-start | bytes 393224 | tf_op jit(solution)/shard_map/ppermute | solution.py:44
  8.6 9.0 %collective-permute-start = (bf16[256,256]{1,0:T(8,128)(2,1)S(1)}, bf16[256,256]{1,0:T(8,128)(2,1)S(1)}, u32[]{:S(2)}, u32[]{:S(2)}) collective-permute-start(bf16[256,256]{1,0:T(8,128)(2,1)S(1)} %pad_maximum_fusion.3), channel_id=1, source_target_pairs={{0,16},{1,129},{2,18},{3,131},{4,20},{5,133},{6,22},{7,135},{8,24}... | collective-permute-start | bytes 393224 | tf_op jit(solution)/shard_map/ppermute | solution.py:44
  13.4 4.2 %collective-permute-start.3 = (bf16[128,1024]{1,0:T(8,128)(2,1)S(1)}, bf16[128,1024]{1,0:T(8,128)(2,1)S(1)}, u32[]{:S(2)}, u32[]{:S(2)}) collective-permute-start(bf16[128,1024]{1,0:T(8,128)(2,1)S(1)} %turn.1), channel_id=1, source_target_pairs={{0,1},{1,0},{2,3},{3,2},{4,5},{5,4},{6,7},{7,6},{8,9},{9,8},{10,11... | collective-permute-start | bytes 786440 | tf_op jit(solution)/shard_map/ppermute | solution.py:44
  17.6 31.8 %collective-permute-start.11 = (bf16[512,8192]{1,0:T(8,128)(2,1)}, bf16[512,8192]{1,0:T(8,128)(2,1)}, u32[]{:S(2)}, u32[]{:S(2)}) collective-permute-start(bf16[512,8192]{1,0:T(8,128)(2,1)} %rest_1_.1), channel_id=1, source_target_pairs={{0,1},{1,0},{2,3},{3,2},{4,5},{5,4},{6,7},{7,6},{8,9},{9,8},{10,11... | collective-permute-start | bytes 25165832 | tf_op jit(solution)/shard_map/ppermute | solution.py:44
  18.0 17.4 %collective-permute-start.10 = (bf16[640,256]{1,0:T(8,128)(2,1)S(1)}, bf16[640,256]{1,0:T(8,128)(2,1)S(1)}, u32[]{:S(2)}, u32[]{:S(2)}) collective-permute-start(bf16[640,256]{1,0:T(8,128)(2,1)S(1)} %pad_maximum_fusion.1), channel_id=1, source_target_pairs={{0,4},{1,5},{2,6},{3,7},{4,8},{5,9},{6,10},{7,11},{8,12},{9,13},{1... | collective-permute-start | bytes 983048 | tf_op jit(solution)/shard_map/ppermute | solution.py:44
  19.3 19.3 %collective-permute-start.9 = (bf16[640,256]{1,0:T(8,128)(2,1)S(1)}, bf16[640,256]{1,0:T(8,128)(2,1)S(1)}, u32[]{:S(2)}, u32[]{:S(2)}) collective-permute-start(bf16[640,256]{1,0:T(8,128)(2,1)S(1)} %pad_maximum_fusion.1), channel_id=1, source_target_pairs={{0,12},{1,13},{2,14},{3,15},{4,0},{5,1},{6,2},{7,3},{8,4},{9,5},{1... | collective-permute-start | bytes 983048 | tf_op jit(solution)/shard_map/ppermute | solution.py:44
  22.2 13.2 %collective-permute-start.4 = (bf16[512,256]{1,0:T(8,128)(2,1)S(1)}, bf16[512,256]{1,0:T(8,128)(2,1)S(1)}, u32[]{:S(2)}, u32[]{:S(2)}) collective-permute-start(bf16[512,256]{1,0:T(8,128)(2,1)S(1)} %pad_maximum_fusion.2.rest_1_), channel_id=1, source_target_pairs={{0,32},{1,225},{2,34},{3,227},{4,36},{5,229},{6,38},{7,231},{8,40}... | collective-permute-start | bytes 786440 | tf_op jit(solution)/shard_map/ppermute | solution.py:44
  25.6 20.6 %collective-permute-start.8 = (bf16[640,256]{1,0:T(8,128)(2,1)S(1)}, bf16[640,256]{1,0:T(8,128)(2,1)S(1)}, u32[]{:S(2)}, u32[]{:S(2)}) collective-permute-start(bf16[640,256]{1,0:T(8,128)(2,1)S(1)} %pad_maximum_fusion.1), channel_id=1, source_target_pairs={{0,8},{1,9},{2,10},{3,11},{4,12},{5,13},{6,14},{7,15},{8,0},{9,1},... | collective-permute-start | bytes 983048 | tf_op jit(solution)/shard_map/ppermute | solution.py:44
  35.4 14.0 %collective-permute-start.7 = (bf16[512,256]{1,0:T(8,128)(2,1)S(1)}, bf16[512,256]{1,0:T(8,128)(2,1)S(1)}, u32[]{:S(2)}, u32[]{:S(2)}) collective-permute-start(bf16[512,256]{1,0:T(8,128)(2,1)S(1)} %collective-permute-done.4.rest_0_), channel_id=1, source_target_pairs={{0,4},{1,5},{2,6},{3,7},{4,8},{5,9},{6,10},{7,11},{8,12},{9,13},{1... | collective-permute-start | bytes 786440 | tf_op jit(solution)/shard_map/ppermute | solution.py:44
  35.4 16.1 %collective-permute-start.6 = (bf16[512,256]{1,0:T(8,128)(2,1)S(1)}, bf16[512,256]{1,0:T(8,128)(2,1)S(1)}, u32[]{:S(2)}, u32[]{:S(2)}) collective-permute-start(bf16[512,256]{1,0:T(8,128)(2,1)S(1)} %collective-permute-done.4.rest_0_), channel_id=1, source_target_pairs={{0,12},{1,13},{2,14},{3,15},{4,0},{5,1},{6,2},{7,3},{8,4},{9,5},{1... | collective-permute-start | bytes 786440 | tf_op jit(solution)/shard_map/ppermute | solution.py:44
  38.6 15.0 %collective-permute-start.5 = (bf16[512,256]{1,0:T(8,128)(2,1)S(1)}, bf16[512,256]{1,0:T(8,128)(2,1)S(1)}, u32[]{:S(2)}, u32[]{:S(2)}) collective-permute-start(bf16[512,256]{1,0:T(8,128)(2,1)S(1)} %collective-permute-done.4.rest_0_), channel_id=1, source_target_pairs={{0,8},{1,9},{2,10},{3,11},{4,12},{5,13},{6,14},{7,15},{8,0},{9,1},... | collective-permute-start | bytes 786440 | tf_op jit(solution)/shard_map/ppermute | solution.py:44
  43.6 15.1 %slice-start = ((s8[8388608]{0:T(1024)(128)(4,1)}), s8[4194304]{0:T(1024)(128)(4,1)S(1)}, s32[]{:S(2)}) async-start(s8[8388608]{0:T(1024)(128)(4,1)} %bitcast.13), calls=%async_computation | async-start | bytes 8388608
  49.4 9.4 %slice-start.1 = ((s8[8388608]{0:T(1024)(128)(4,1)}), s8[4194304]{0:T(1024)(128)(4,1)S(1)}, s32[]{:S(2)}) async-start(s8[8388608]{0:T(1024)(128)(4,1)} %bitcast.13), calls=%async_computation.1 | async-start | bytes 8388608
  55.9 2.8 %collective-permute-start.12 = (f32[136,2048]{1,0:T(8,128)S(1)}, f32[136,2048]{1,0:T(8,128)S(1)}, u32[]{:S(2)}, u32[]{:S(2)}) collective-permute-start(f32[136,2048]{1,0:T(8,128)S(1)} %attend.15.rest_0_), channel_id=1, source_target_pairs={{0,1},{1,0},{2,3},{3,2},{4,5},{5,4},{6,7},{7,6},{8,9},{9,8},{10,11... | collective-permute-start | bytes 3342344 | tf_op jit(solution)/shard_map/ppermute | solution.py:44
  60.4 12.7 %collective-permute-start.16 = (bf16[256,512]{1,0:T(8,128)(2,1)S(1)}, bf16[256,512]{1,0:T(8,128)(2,1)S(1)}, u32[]{:S(2)}, u32[]{:S(2)}) collective-permute-start(bf16[256,512]{1,0:T(8,128)(2,1)S(1)} %get-tuple-element.36), channel_id=1, source_target_pairs={{0,2},{1,3},{2,0},{3,1},{4,6},{5,7},{6,4},{7,5},{8,10},{9,11},{10,... | collective-permute-start | bytes 786440 | tf_op jit(solution)/shard_map/ppermute | solution.py:44
  64.4 12.4 %collective-permute-start.15 = (bf16[256,512]{1,0:T(8,128)(2,1)S(1)}, bf16[256,512]{1,0:T(8,128)(2,1)S(1)}, u32[]{:S(2)}, u32[]{:S(2)}) collective-permute-start(bf16[256,512]{1,0:T(8,128)(2,1)S(1)} %get-tuple-element.35), channel_id=1, source_target_pairs={{0,2},{1,3},{2,0},{3,1},{4,6},{5,7},{6,4},{7,5},{8,10},{9,11},{10,... | collective-permute-start | bytes 786440 | tf_op jit(solution)/shard_map/ppermute | solution.py:44
  66.6 15.8 %collective-permute-start.14 = (bf16[256,512]{1,0:T(8,128)(2,1)S(1)}, bf16[256,512]{1,0:T(8,128)(2,1)S(1)}, u32[]{:S(2)}, u32[]{:S(2)}) collective-permute-start(bf16[256,512]{1,0:T(8,128)(2,1)S(1)} %get-tuple-element.34), channel_id=1, source_target_pairs={{0,2},{1,3},{2,0},{3,1},{4,6},{5,7},{6,4},{7,5},{8,10},{9,11},{10,... | collective-permute-start | bytes 786440 | tf_op jit(solution)/shard_map/ppermute | solution.py:44
  68.0 19.2 %collective-permute-start.13 = (bf16[256,512]{1,0:T(8,128)(2,1)S(1)}, bf16[256,512]{1,0:T(8,128)(2,1)S(1)}, u32[]{:S(2)}, u32[]{:S(2)}) collective-permute-start(bf16[256,512]{1,0:T(8,128)(2,1)S(1)} %get-tuple-element.33), channel_id=1, source_target_pairs={{0,2},{1,3},{2,0},{3,1},{4,6},{5,7},{6,4},{7,5},{8,10},{9,11},{10,... | collective-permute-start | bytes 786440 | tf_op jit(solution)/shard_map/ppermute | solution.py:44
